TPU v7x, 256 devices: a whole 4x4x8 slice. The times are simulated.
256 devices in a mesh: store: 128 (over y_hi, z, x, core), pair: 2 (over y_lo).
Axes of the slice: x: 4, y: 4 (y_hi: 2, y_lo: 2; y = y_hi * 2 + y_lo), z: 8, core: 2. Of those that a mesh axis runs over, the one named last changes fastest.
Arguments:
- queries: bfloat16 [128, 2, 2, 128, 8192], P('store', 'pair'), may hold values from -6 to 6
- suffix_keys: bfloat16 [128, 2, 2, 128, 1024], P('store', 'pair'), may hold values from -6 to 6
- suffix_values: bfloat16 [128, 2, 2, 128, 1024], P('store', 'pair'), may hold values from -6 to 6
- page_keys: bfloat16 [8192, 8, 1024], P('store'), may hold values from -6 to 6
- page_values: bfloat16 [8192, 8, 1024], P('store'), may hold values from -6 to 6
- leaf_parent: int32 [64], replicated, may hold values from 0 to 15
- node_pages: int32 [81], replicated, may hold values from 1 to 64, as said below
- page_slot: int32 [81, 64], replicated, may hold values from 0 to 8191, as said below
- request_leaf: int32 [128], replicated, may hold values from 0 to 63
- prefix_len: int32 [128], replicated, may hold values from 1 to 1024, as said below
Outputs:
- attended: bfloat16 [128, 2, 2, 128, 8192], P('store', 'pair')
Inputs may be any that keep to these rules, and one draw needn't show every extreme that they name: `node_pages`: entry 0 is the root with at most 32 pages, entries 1 to 16 are the middle nodes with at most 32 pages, the others are the leaves with at most 64. `page_slot`: entries [n, i] with i at or above node n's page count are 0; all other entries are distinct; place g lies on store index g // 64; the pages of one request's path lie at most 1 to a store index, and some request's path reaches 1. `prefix_len`: at least half of the request's path tokens and at most all of them.
All inputs are finite; a program needn't handle non-finite values.
Results may differ from a plain program's by a relative error of at most 0.008.
Values may be sent and summed in bfloat16 or wider, within the bound.
A program may use at most 128 MiB of HBM per device.

v0:
```python
import jax
import jax.numpy as jnp
from jax import lax
from jax.sharding import PartitionSpec as P

QH = 64
KVH = 8
HD = 128
PAGE = 8
PREFIX_PG = 128


def swapped(array, axis, bit):
    return lax.ppermute(array, axis, [(i, i ^ 1 << bit) for i in range(lax.axis_size(axis))])


def path_table(leaf_parent, node_pages, page_slot, request_leaf, prefix_len):
    mids = node_pages.shape[0] - 1 - leaf_parent.shape[0]
    row_width = page_slot.shape[1]
    leaf_node = 1 + mids + request_leaf
    mid_node = 1 + jnp.take(leaf_parent, request_leaf)
    root_count = node_pages[0]
    mid_count = jnp.take(node_pages, mid_node)[:, None]
    leaf_count = jnp.take(node_pages, leaf_node)[:, None]
    page_order = jnp.arange(PREFIX_PG, dtype=jnp.int32)[None, :]
    in_root = page_order < root_count
    in_mid = page_order < root_count + mid_count
    node_ids = jnp.where(in_root, 0, jnp.where(in_mid, mid_node[:, None], leaf_node[:, None]))
    within = jnp.where(
        in_root,
        page_order,
        jnp.where(in_mid, page_order - root_count, page_order - root_count - mid_count),
    )
    in_use = (page_order < root_count + mid_count + leaf_count) & (
        page_order * PAGE < prefix_len[:, None]
    )
    within = jnp.where(in_use, within, 0)
    page_ids = jnp.take(page_slot.reshape(-1), node_ids * row_width + within)
    return (jnp.where(in_use, page_ids, 0), in_use)


def attend_block(state, head_queries, block_keys, block_values, allowed, score_scale):
    running_max, running_sum, weighted = state
    scores = (
        jnp.einsum("hqd,khd->hqk", head_queries, block_keys, preferred_element_type=jnp.float32)
        * score_scale
    )
    scores = jnp.where(allowed, scores, -1e30)
    new_max = jnp.maximum(running_max, jnp.max(scores, axis=-1))
    factor = jnp.exp(running_max - new_max)
    weights = jnp.exp(scores - new_max[..., None])
    running_sum = running_sum * factor + jnp.sum(weights, axis=-1)
    weighted = weighted * factor[..., None] + jnp.einsum(
        "hqk,khd->hqd",
        weights.astype(jnp.bfloat16),
        block_values,
        preferred_element_type=jnp.float32,
    )
    return (new_max, running_sum, weighted)


def mirror_pos(pair_index, pairs, block_rows):
    block_ids = jnp.stack([pair_index, 2 * pairs - 1 - pair_index])
    return (
        block_ids[:, None] * block_rows + jnp.arange(block_rows, dtype=jnp.int32)[None, :]
    ).reshape(-1)


def local(
    queries,
    suffix_keys,
    suffix_values,
    page_keys,
    page_values,
    leaf_parent,
    node_pages,
    page_slot,
    request_leaf,
    prefix_len,
):
    stores = lax.axis_size("store")
    pairs = lax.axis_size("pair")
    store_index = lax.axis_index("store")
    pair_index = lax.axis_index("pair")
    pages_dev = page_keys.shape[0]
    kv_width = page_keys.shape[2]
    capacity = PREFIX_PG // stores
    group_size = QH // KVH
    block_rows = queries.shape[3]
    score_scale = HD ** (-0.5)
    page_ids, in_use = path_table(leaf_parent, node_pages, page_slot, request_leaf, prefix_len)
    holder = page_ids // pages_dev
    local_row = page_ids % pages_dev
    is_mine = in_use & (holder == store_index)
    mine_rank = jnp.cumsum(is_mine.astype(jnp.int32), axis=1) - 1
    chosen = is_mine[:, :, None] & (
        mine_rank[:, :, None] == jnp.arange(capacity, dtype=jnp.int32)[None, None, :]
    )
    send_rows = jnp.sum(jnp.where(chosen, local_row[:, :, None], 0), axis=1)
    send_used = jnp.any(chosen, axis=1)[:, :, None, None]
    sent_keys = jnp.where(send_used, jnp.take(page_keys, send_rows, axis=0), 0)
    sent_values = jnp.where(send_used, jnp.take(page_values, send_rows, axis=0), 0)
    recv_keys, recv_values = (
        lax.all_to_all(sent_keys, "store", split_axis=0, concat_axis=0, tiled=True),
        lax.all_to_all(sent_values, "store", split_axis=0, concat_axis=0, tiled=True),
    )
    flat_keys = recv_keys.reshape(stores * capacity, PAGE, kv_width)
    flat_values = recv_values.reshape(stores * capacity, PAGE, kv_width)
    partner_keys, partner_values = swapped((suffix_keys, suffix_values), "pair", 0)
    my_pages = lax.dynamic_index_in_dim(page_ids, store_index, 0, keepdims=False)
    my_use = lax.dynamic_index_in_dim(in_use, store_index, 0, keepdims=False)
    my_length = lax.dynamic_index_in_dim(prefix_len, store_index, 0, keepdims=False)
    my_holder = my_pages // pages_dev
    same_holder = (my_holder[:, None] == jnp.arange(stores, dtype=jnp.int32)[None, :]) & my_use[
        :, None
    ]
    prior_count = jnp.cumsum(same_holder.astype(jnp.int32), axis=0) - 1
    holder_rank = jnp.sum(jnp.where(same_holder, prior_count, 0), axis=1)
    buffer_row = jnp.where(my_use, my_holder * capacity + holder_rank, 0)
    query_count = queries.shape[0] * queries.shape[1] * queries.shape[2] * block_rows
    head_queries = jnp.transpose(
        queries.reshape(query_count, KVH, group_size, HD), (1, 0, 2, 3)
    ).reshape(KVH, query_count * group_size, HD)
    row_count = query_count * group_size
    query_pos = mirror_pos(pair_index, pairs, block_rows)
    partner_pos = mirror_pos(1 - pair_index, pairs, block_rows)
    state = (
        jnp.full((KVH, row_count), -1e30, jnp.float32),
        jnp.zeros((KVH, row_count), jnp.float32),
        jnp.zeros((KVH, row_count, HD), jnp.float32),
    )
    own_allowed = jnp.repeat(query_pos[:, None] >= query_pos[None, :], group_size, axis=0)[None]
    state = attend_block(
        state,
        head_queries,
        suffix_keys.reshape(-1, KVH, HD),
        suffix_values.reshape(-1, KVH, HD),
        own_allowed,
        score_scale,
    )
    partner_allowed = jnp.repeat(query_pos[:, None] >= partner_pos[None, :], group_size, axis=0)[
        None
    ]
    state = attend_block(
        state,
        head_queries,
        partner_keys.reshape(-1, KVH, HD),
        partner_values.reshape(-1, KVH, HD),
        partner_allowed,
        score_scale,
    )
    tokens = PREFIX_PG * PAGE
    block_size = min(256, tokens)
    slot_match = (
        buffer_row[None, :] == jnp.arange(stores * capacity, dtype=jnp.int32)[:, None]
    ) & my_use[None, :]
    page_of = jnp.sum(
        jnp.where(slot_match, jnp.arange(PREFIX_PG, dtype=jnp.int32)[None, :], 0), axis=1
    )
    filled = jnp.any(slot_match, axis=1)
    token_pos = (page_of[:, None] * PAGE + jnp.arange(PAGE, dtype=jnp.int32)[None, :]).reshape(-1)
    usable = jnp.repeat(filled, PAGE) & (token_pos < my_length)
    all_keys = flat_keys.reshape(tokens, KVH, HD)
    all_values = flat_values.reshape(tokens, KVH, HD)

    def visit(block_index, carried):
        block_start = block_index * block_size
        block_keys = lax.dynamic_slice_in_dim(all_keys, block_start, block_size, 0)
        block_values = lax.dynamic_slice_in_dim(all_values, block_start, block_size, 0)
        allowed = lax.dynamic_slice_in_dim(usable, block_start, block_size, 0)[None, None, :]
        return attend_block(carried, head_queries, block_keys, block_values, allowed, score_scale)

    state = lax.fori_loop(0, tokens // block_size, visit, state)
    running_max, running_sum, weighted = state
    result = (weighted / running_sum[..., None]).reshape(KVH, query_count, group_size, HD)
    return jnp.transpose(result, (1, 0, 2, 3)).astype(jnp.bfloat16).reshape(queries.shape)


def solution(mesh):
    return jax.shard_map(
        local,
        mesh=mesh,
        in_specs=(
            P("store", "pair", None, None, None),
            P("store", "pair", None, None, None),
            P("store", "pair", None, None, None),
            P("store", None, None),
            P("store", None, None),
            P(),
            P(),
            P(),
            P(),
            P(),
        ),
        out_specs=P("store", "pair", None, None, None),
        check_vma=False,
    )
```

profile of v0, /device:TPU:1, one launch (start us, length us, event | category | flops | bytes accessed | tf_op | source)
XLA Modules:
  0.0 398.1 jit_solution(766093429280210326)
XLA Ops:
  12.1 90.5 %gather_fusion.1 = s32[16384]{0:T(1024)S(1)} fusion(s32[5184]{0:T(1024)S(1)} %reshape.1190, s32[16384]{0:T(1024)S(1)} %bitcast_clamp_fusion), kind=kCustom, calls=%fused_computation.5 | custom fusion | bytes 196608 | tf_op jit(solution)/shard_map/jit(_take)/gather | solution.py:38
  111.4 16.8 %all-to-all-start = ((bf16[128,1,8,1024]{3,2,1,0:T(8,128)(2,1)}), bf16[128,1,8,1024]{3,2,1,0:T(8,128)(2,1)S(1)}, u32[]{:S(2)}, u32[]{:S(2)}) async-start(bf16[128,1,8,1024]{3,2,1,0:T(8,128)(2,1)} %get-tuple-element.203), calls=%async_computation | async-start | bytes 4194304 | tf_op jit(solution)/shard_map/all_to_all | solution.py:104
  149.4 7.8 %fusion.16 = (f32[8,2048]{1,0:T(8,128)S(1)}, f32[8,2048,256]{1,2,0:T(8,128)}) fusion(pred[2048,256]{0,1:T(8,128)(4,1)S(1)} %copy.37, bf16[256,8,128]{2,1,0:T(8,128)(2,1)S(1)} %bitcast.156, bf16[256,8,8,128]{3,2,1,0:T(8,128)(2,1)S(1)} %bitcast.146), kind=kOutput, calls=%fused_computation.31 | convolution fusion | flops 1086308352 | bytes 22085632 | tf_op jit(solution)/shard_map/hqd,khd->hqk/dot_general | solution.py:45
  159.5 7.9 %fusion.17 = (f32[8,2048]{1,0:T(8,128)S(1)}, f32[8,2048,256]{1,2,0:T(8,128)}) fusion(pred[2048,256]{0,1:T(8,128)(4,1)S(1)} %copy.40, bf16[256,8,128]{2,1,0:T(8,128)(2,1)S(1)} %bitcast.157, bf16[256,8,8,128]{3,2,1,0:T(8,128)(2,1)S(1)} %bitcast.147), kind=kOutput, calls=%fused_computation.32 | convolution fusion | flops 1086308352 | bytes 22085632 | tf_op jit(solution)/shard_map/hqd,khd->hqk/dot_general | solution.py:45
  168.0 9.3 %fusion.21 = f32[8,2048]{1,0:T(8,128)S(1)} fusion(f32[8,2048,256]{1,2,0:T(8,128)} %get-tuple-element.211, f32[8,2048]{1,0:T(8,128)S(1)} %get-tuple-element.277, pred[2048,256]{0,1:T(8,128)(4,1)S(1)} %copy.40), kind=kLoop, calls=%fused_computation.36 | loop fusion | flops 16760832 | bytes 17432576 | tf_op jit(solution)/shard_map/reduce_sum | solution.py:52
  183.4 8.3 %all-to-all-start.1 = ((bf16[128,1,8,1024]{3,2,1,0:T(8,128)(2,1)}), bf16[128,1,8,1024]{3,2,1,0:T(8,128)(2,1)}, u32[]{:S(2)}, u32[]{:S(2)}) async-start(bf16[128,1,8,1024]{3,2,1,0:T(8,128)(2,1)} %get-tuple-element.202), calls=%async_computation.1 | async-start | bytes 4194304 | tf_op jit(solution)/shard_map/all_to_all | solution.py:105
  191.8 9.4 %fusion.19 = f32[8,2048]{1,0:T(8,128)S(1)} fusion(f32[8,2048,256]{1,2,0:T(8,128)} %get-tuple-element.209, f32[8,2048]{1,0:T(8,128)S(1)} %get-tuple-element.200, pred[2048,256]{0,1:T(8,128)(4,1)} %copy-done.5), kind=kLoop, calls=%fused_computation.34 | loop fusion | flops 16760832 | bytes 17432576 | tf_op jit(solution)/shard_map/reduce_sum | solution.py:52
  202.1 8.6 %fusion.24 = f32[8,2048,128]{2,1,0:T(8,128)S(1)} fusion(f32[8,2048,256]{1,2,0:T(8,128)} %get-tuple-element.209, f32[8,2048]{1,0:T(8,128)S(1)} %get-tuple-element.200, pred[2048,256]{0,1:T(8,128)(4,1)} %copy-done.5, bf16[256,8,128]{2,1,0:T(8,128)(2,1)} %bitcast.155), kind=kOutput, calls=%fused_computation.38 | convolution fusion | flops 1090519040 | bytes 26279936 | tf_op jit(solution)/shard_map/hqk,khd->hqd/dot_general | solution.py:53
  210.7 13.7 %multiply_add_fusion.2 = f32[8,2048,128]{2,1,0:T(8,128)} fusion(f32[8,2048,128]{2,1,0:T(8,128)S(1)} %fusion.24, f32[8,2048]{1,0:T(8,128)S(1)} %get-tuple-element.193, f32[8,2048]{1,0:T(8,128)S(1)} %get-tuple-element.198, f32[8,2048,256]{1,2,0:T(8,128)} %get-tuple-element.211, f32[8,2048]{1,0:T(8,128)S(1)} %get-tuple-element.277, ...), kind=kOutput, calls=%fused_computation.40 | convolution fusion | flops 1096810496 | bytes 34799616 | tf_op jit(solution)/shard_map/hqk,khd->hqd/dot_general | solution.py:53
  225.0 21.8 %all-to-all-done.1 = bf16[128,1,8,1024]{3,2,1,0:T(8,128)(2,1)} async-done(((bf16[128,1,8,1024]{3,2,1,0:T(8,128)(2,1)}), bf16[128,1,8,1024]{3,2,1,0:T(8,128)(2,1)}, u32[]{:S(2)}, u32[]{:S(2)}) %all-to-all-start.1) | async-done | bytes 2097184 | tf_op jit(solution)/shard_map/all_to_all | solution.py:105
  250.3 133.3 %while.17 = (s32[]{:T(128)}, f32[8,2048]{1,0:T(8,128)S(1)}, f32[8,2048]{1,0:T(8,128)S(1)}, f32[8,2048,128]{2,1,0:T(8,128)}, pred[1024]{0:T(1024)(128)(4,1)S(1)},...) while((s32[]{:T(128)}, f32[8,2048]{1,0:T(8,128)S(1)}, ...), condition=%wide.region_14.17_spmd, body=%wide.region_11.16_spmd.sunk | while | flops 2197848064 | bytes 75498920 | solution.py:173
  251.7 9.3 %bitcast_reduce_fusion.2 = (f32[8,2048]{1,0:T(8,128)S(1)}, f32[8,256,2048]{2,1,0:T(8,128)}) fusion(pred[256]{0:T(512)(128)(4,1)S(1)} %dynamic_slice.51, bf16[8,2048,128]{2,1,0:T(8,128)(2,1)} %get-tuple-element.306, bf16[256,8,128]{2,1,0:T(8,128)(2,1)S(1)} %get-tuple-element.270), kind=kOutput, calls=%fused_computation.7.clone.1 | convolution fusion | flops 1086308352 | bytes 21561600 | tf_op jit(solution)/shard_map/while/body/eval_jaxpr/hqd,khd->hqk/dot_general | solution.py:45
  261.1 9.3 %fusion.86 = f32[8,2048]{1,0:T(8,128)S(1)} fusion(f32[8,256,2048]{2,1,0:T(8,128)} %get-tuple-element.272, f32[8,2048]{1,0:T(8,128)S(1)} %max.23, pred[256]{0:T(512)(128)(4,1)S(1)} %dynamic_slice.51), kind=kLoop, calls=%fused_computation.11.clone.1 | loop fusion | flops 16760832 | bytes 16908544 | tf_op jit(solution)/shard_map/while/body/eval_jaxpr/reduce_sum | solution.py:52
  270.4 13.4 %multiply_add_fusion.7 = f32[8,2048,128]{2,1,0:T(8,128)} fusion(f32[8,2048,128]{2,1,0:T(8,128)} %get-tuple-element.291, f32[8,2048]{1,0:T(8,128)S(1)} %get-tuple-element.274, f32[8,256,2048]{2,1,0:T(8,128)} %get-tuple-element.272, f32[8,2048]{1,0:T(8,128)S(1)} %max.23, pred[256]{0:T(512)(128)(4,1)S(1)} %dynamic_slice.51, ...), kind=kOutput, calls=%fused_computation.13.clone.1 | convolution fusion | flops 1094713344 | bytes 34210048 | tf_op jit(solution)/shard_map/while/body/eval_jaxpr/hqk,khd->hqd/dot_general | solution.py:53
  285.0 9.4 %bitcast_reduce_fusion.2 = (f32[8,2048]{1,0:T(8,128)S(1)}, f32[8,256,2048]{2,1,0:T(8,128)}) fusion(pred[256]{0:T(512)(128)(4,1)S(1)} %dynamic_slice.51, bf16[8,2048,128]{2,1,0:T(8,128)(2,1)} %get-tuple-element.306, bf16[256,8,128]{2,1,0:T(8,128)(2,1)S(1)} %get-tuple-element.270), kind=kOutput, calls=%fused_computation.7.clone.1 | convolution fusion | flops 1086308352 | bytes 21561600 | tf_op jit(solution)/shard_map/while/body/eval_jaxpr/hqd,khd->hqk/dot_general | solution.py:45
  294.3 9.3 %fusion.86 = f32[8,2048]{1,0:T(8,128)S(1)} fusion(f32[8,256,2048]{2,1,0:T(8,128)} %get-tuple-element.272, f32[8,2048]{1,0:T(8,128)S(1)} %max.23, pred[256]{0:T(512)(128)(4,1)S(1)} %dynamic_slice.51), kind=kLoop, calls=%fused_computation.11.clone.1 | loop fusion | flops 16760832 | bytes 16908544 | tf_op jit(solution)/shard_map/while/body/eval_jaxpr/reduce_sum | solution.py:52
  303.7 13.4 %multiply_add_fusion.7 = f32[8,2048,128]{2,1,0:T(8,128)} fusion(f32[8,2048,128]{2,1,0:T(8,128)} %get-tuple-element.291, f32[8,2048]{1,0:T(8,128)S(1)} %get-tuple-element.274, f32[8,256,2048]{2,1,0:T(8,128)} %get-tuple-element.272, f32[8,2048]{1,0:T(8,128)S(1)} %max.23, pred[256]{0:T(512)(128)(4,1)S(1)} %dynamic_slice.51, ...), kind=kOutput, calls=%fused_computation.13.clone.1 | convolution fusion | flops 1094713344 | bytes 34210048 | tf_op jit(solution)/shard_map/while/body/eval_jaxpr/hqk,khd->hqd/dot_general | solution.py:53
  318.3 9.4 %bitcast_reduce_fusion.2 = (f32[8,2048]{1,0:T(8,128)S(1)}, f32[8,256,2048]{2,1,0:T(8,128)}) fusion(pred[256]{0:T(512)(128)(4,1)S(1)} %dynamic_slice.51, bf16[8,2048,128]{2,1,0:T(8,128)(2,1)} %get-tuple-element.306, bf16[256,8,128]{2,1,0:T(8,128)(2,1)S(1)} %get-tuple-element.270), kind=kOutput, calls=%fused_computation.7.clone.1 | convolution fusion | flops 1086308352 | bytes 21561600 | tf_op jit(solution)/shard_map/while/body/eval_jaxpr/hqd,khd->hqk/dot_general | solution.py:45
  327.6 9.3 %fusion.86 = f32[8,2048]{1,0:T(8,128)S(1)} fusion(f32[8,256,2048]{2,1,0:T(8,128)} %get-tuple-element.272, f32[8,2048]{1,0:T(8,128)S(1)} %max.23, pred[256]{0:T(512)(128)(4,1)S(1)} %dynamic_slice.51), kind=kLoop, calls=%fused_computation.11.clone.1 | loop fusion | flops 16760832 | bytes 16908544 | tf_op jit(solution)/shard_map/while/body/eval_jaxpr/reduce_sum | solution.py:52
  336.9 13.4 %multiply_add_fusion.7 = f32[8,2048,128]{2,1,0:T(8,128)} fusion(f32[8,2048,128]{2,1,0:T(8,128)} %get-tuple-element.291, f32[8,2048]{1,0:T(8,128)S(1)} %get-tuple-element.274, f32[8,256,2048]{2,1,0:T(8,128)} %get-tuple-element.272, f32[8,2048]{1,0:T(8,128)S(1)} %max.23, pred[256]{0:T(512)(128)(4,1)S(1)} %dynamic_slice.51, ...), kind=kOutput, calls=%fused_computation.13.clone.1 | convolution fusion | flops 1094713344 | bytes 34210048 | tf_op jit(solution)/shard_map/while/body/eval_jaxpr/hqk,khd->hqd/dot_general | solution.py:53
  351.6 9.4 %bitcast_reduce_fusion.2 = (f32[8,2048]{1,0:T(8,128)S(1)}, f32[8,256,2048]{2,1,0:T(8,128)}) fusion(pred[256]{0:T(512)(128)(4,1)S(1)} %dynamic_slice.51, bf16[8,2048,128]{2,1,0:T(8,128)(2,1)} %get-tuple-element.306, bf16[256,8,128]{2,1,0:T(8,128)(2,1)S(1)} %get-tuple-element.270), kind=kOutput, calls=%fused_computation.7.clone.1 | convolution fusion | flops 1086308352 | bytes 21561600 | tf_op jit(solution)/shard_map/while/body/eval_jaxpr/hqd,khd->hqk/dot_general | solution.py:45
  360.9 9.3 %fusion.86 = f32[8,2048]{1,0:T(8,128)S(1)} fusion(f32[8,256,2048]{2,1,0:T(8,128)} %get-tuple-element.272, f32[8,2048]{1,0:T(8,128)S(1)} %max.23, pred[256]{0:T(512)(128)(4,1)S(1)} %dynamic_slice.51), kind=kLoop, calls=%fused_computation.11.clone.1 | loop fusion | flops 16760832 | bytes 16908544 | tf_op jit(solution)/shard_map/while/body/eval_jaxpr/reduce_sum | solution.py:52
  370.2 13.4 %multiply_add_fusion.7 = f32[8,2048,128]{2,1,0:T(8,128)} fusion(f32[8,2048,128]{2,1,0:T(8,128)} %get-tuple-element.291, f32[8,2048]{1,0:T(8,128)S(1)} %get-tuple-element.274, f32[8,256,2048]{2,1,0:T(8,128)} %get-tuple-element.272, f32[8,2048]{1,0:T(8,128)S(1)} %max.23, pred[256]{0:T(512)(128)(4,1)S(1)} %dynamic_slice.51, ...), kind=kOutput, calls=%fused_computation.13.clone.1 | convolution fusion | flops 1094713344 | bytes 34210048 | tf_op jit(solution)/shard_map/while/body/eval_jaxpr/hqk,khd->hqd/dot_general | solution.py:53
  390.6 7.3 %reshape.1191 = bf16[1,1,2,128,8192]{4,3,2,1,0:T(8,128)(2,1)} reshape(bf16[256,8,8,128]{3,2,1,0:T(8,128)(2,1)} %copy_bitcast_fusion) | data formatting | bytes 8388608 | tf_op jit(solution)/shard_map/reshape | solution.py:176
  (103 shorter events, 67.8 us)
Async XLA Ops:
  0.0 103.8 %copy-start = (bf16[64,8,1024]{2,1,0:T(8,128)(2,1)S(1)}, bf16[64,8,1024]{2,1,0:T(8,128)(2,1)}, u32[]{:S(2)}) copy-start(bf16[64,8,1024]{2,1,0:T(8,128)(2,1)} %param.19) | copy-start | bytes 3145732
  0.0 157.1 %collective-permute-start = (bf16[1,1,2,128,1024]{4,3,2,1,0:T(8,128)(2,1)}, bf16[1,1,2,128,1024]{4,3,2,1,0:T(8,128)(2,1)}, u32[]{:S(2)}, u32[]{:S(2)}) collective-permute-start(bf16[1,1,2,128,1024]{4,3,2,1,0:T(8,128)(2,1)} %param.17), channel_id=1, source_target_pairs={{0,1},{1,0},{2,3},{3,2},{4,5},{5,4},{6,7},{7,6},{8,9},{9,8},{10,11... | collective-permute-start | bytes 1572872 | tf_op jit(solution)/shard_map/ppermute | solution.py:14
  2.1 156.2 %collective-permute-start.1 = (bf16[1,1,2,128,1024]{4,3,2,1,0:T(8,128)(2,1)}, bf16[1,1,2,128,1024]{4,3,2,1,0:T(8,128)(2,1)}, u32[]{:S(2)}, u32[]{:S(2)}) collective-permute-start(bf16[1,1,2,128,1024]{4,3,2,1,0:T(8,128)(2,1)} %param.18), channel_id=1, source_target_pairs={{0,1},{1,0},{2,3},{3,2},{4,5},{5,4},{6,7},{7,6},{8,9},{9,8},{10,11... | collective-permute-start | bytes 1572872 | tf_op jit(solution)/shard_map/ppermute | solution.py:14
  12.1 90.6 %copy-start.9 = (s32[128]{0:T(128)S(1)}, s32[128]{0:T(128)}, u32[]{:S(2)}) copy-start(s32[128]{0:T(128)} %param.25) | copy-start | bytes 1540
  111.4 72.0 %all-to-all-start = ((bf16[128,1,8,1024]{3,2,1,0:T(8,128)(2,1)}), bf16[128,1,8,1024]{3,2,1,0:T(8,128)(2,1)S(1)}, u32[]{:S(2)}, u32[]{:S(2)}) async-start(bf16[128,1,8,1024]{3,2,1,0:T(8,128)(2,1)} %get-tuple-element.203), calls=%async_computation | async-start | bytes 4194304 | tf_op jit(solution)/shard_map/all_to_all | solution.py:104
  138.1 19.1 %copy-start.5 = (pred[2048,256]{0,1:T(8,128)(4,1)}, pred[2048,256]{0,1:T(8,128)(4,1)S(1)}, u32[]{:S(2)}) copy-start(pred[2048,256]{0,1:T(8,128)(4,1)S(1)} %copy.37) | copy-start | bytes 1572868
  144.3 5.1 %copy-start.2 = (bf16[32,8,64,128]{3,2,1,0:T(8,128)(2,1)S(1)}, bf16[32,8,64,128]{3,2,1,0:T(8,128)(2,1)}, u32[]{:S(2)}) copy-start(bf16[32,8,64,128]{3,2,1,0:T(8,128)(2,1)} %copy.57) | copy-start | bytes 12582916
  144.3 5.1 %copy-start.6 = (bf16[32,8,8,128]{3,2,1,0:T(8,128)(2,1)S(1)}, bf16[32,8,8,128]{3,2,1,0:T(8,128)(2,1)}, u32[]{:S(2)}) copy-start(bf16[32,8,8,128]{3,2,1,0:T(8,128)(2,1)} %copy.58) | copy-start | bytes 1572868
  157.1 10.2 %copy-start.7 = (f32[8,2048]{1,0:T(8,128)}, f32[8,2048]{1,0:T(8,128)S(1)}, u32[]{:S(2)}) copy-start(f32[8,2048]{1,0:T(8,128)S(1)} %get-tuple-element.208) | copy-start | bytes 196612
  167.3 0.6 copy-start.8
  183.4 17.7 %copy-start.3 = (bf16[128,1,8,1024]{3,2,1,0:T(8,128)(2,1)}, bf16[128,1,8,1024]{3,2,1,0:T(8,128)(2,1)S(1)}, u32[]{:S(2)}) copy-start(bf16[128,1,8,1024]{3,2,1,0:T(8,128)(2,1)S(1)} %all-to-all-done) | copy-start | bytes 6291460
  183.4 63.3 %all-to-all-start.1 = ((bf16[128,1,8,1024]{3,2,1,0:T(8,128)(2,1)}), bf16[128,1,8,1024]{3,2,1,0:T(8,128)(2,1)}, u32[]{:S(2)}, u32[]{:S(2)}) async-start(bf16[128,1,8,1024]{3,2,1,0:T(8,128)(2,1)} %get-tuple-element.202), calls=%async_computation.1 | async-start | bytes 4194304 | tf_op jit(solution)/shard_map/all_to_all | solution.py:105
  210.6 13.7 %copy-start.4 = (bf16[128,1,8,1024]{3,2,1,0:T(8,128)(2,1)S(1)}, bf16[128,1,8,1024]{3,2,1,0:T(8,128)(2,1)}, u32[]{:S(2)}) copy-start(bf16[128,1,8,1024]{3,2,1,0:T(8,128)(2,1)} %copy-done.3) | copy-start | bytes 6291460
  383.6 14.2 %copy-start.1 = (bf16[64,8,1024]{2,1,0:T(8,128)(2,1)S(1)}, bf16[64,8,1024]{2,1,0:T(8,128)(2,1)}, u32[]{:S(2)}) copy-start(bf16[64,8,1024]{2,1,0:T(8,128)(2,1)} %param.19) | copy-start | bytes 3145732
where the time goes:
time: 404 us; the launch traced here: 398 us
  local copies, waits for them, and re-layouts  139 us (34%)
  matrix products  129 us (32%)
  other arithmetic  74.3 us (18%)
  waiting for transfers between devices  27.9 us (7%)
  starting transfers between devices  27.3 us (7%)
    gather x1, local copies, waits for them, and re-layouts, path_table(): page_ids = jnp.take(page_slot.reshape(-1), node_ids * row_width + within)  90.5 us
    dot_general x6, matrix products, attend_block(): jnp.einsum('hqk,khd->hqd', weights.astype(jnp.bfloat16), block_values, pr...  75.8 us
    reduce_sum x6, other arithmetic, attend_block(): running_sum = running_sum * factor + jnp.sum(weights, axis=-1)  55.8 us
    dot_general x6, matrix products, attend_block(): jnp.einsum('hqd,khd->hqk', head_queries, block_keys, preferred_element_ty...  53.1 us
    all_to_all x1, waiting for transfers between devices, local(): lax.all_to_all(sent_values, 'store', split_axis=0, concat_axis=0, tiled=T...  21.8 us
    unnamed x28, local copies, waits for them, and re-layouts  17.4 us
    all_to_all x1, starting transfers between devices, local(): lax.all_to_all(sent_keys, 'store', split_axis=0, concat_axis=0, tiled=True)  16.8 us
    all_to_all x1, starting transfers between devices, local(): lax.all_to_all(sent_values, 'store', split_axis=0, concat_axis=0, tiled=T...  8.34 us
  transfers between devices with their start and end apart: 4, of which 2 were waited for; matrix products, arithmetic and copies ran while one was open for 48% of the time, Pallas kernels for 0%

commit v1 on v0

v1 whole, which is shorter than its diff:
```python
import functools

import jax
import jax.numpy as jnp
from jax import lax
from jax.experimental import pallas as pl
from jax.experimental.pallas import tpu as pltpu
from jax.sharding import PartitionSpec as P

QH = 64
KVH = 8
HD = 128
GROUP = QH // KVH
PAGE = 8
PAGES_DEV = 64
SLOTS = 128
CHUNKS = 8
PER_CHUNK = SLOTS // CHUNKS
ROWS = 16
LANES = 512
Z_ORDER = (1, 7, 2, 6, 3, 5, 4, 0)
MESH = pl.DeviceIdType.MESH


def shifted(me, dy, dz, dx, dc):
    yh, z, x, c = me // 64, me // 8 % 8, me // 2 % 4, me % 2
    return (((yh + dy) % 2 * 8 + (z + dz) % 8) * 4 + (x + dx) % 4) * 2 + (c + dc) % 2


def slot_steps():
    d = jnp.arange(SLOTS, dtype=jnp.int32)
    dz = jnp.tile(jnp.repeat(jnp.array(Z_ORDER, jnp.int32), 2), CHUNKS)
    return d // 64, dz, d // 16 % 4, d % 2


def tables(leaf_parent, node_pages, page_slot, request_leaf, prefix_len, me):
    dy, dz, dx, dc = slot_steps()
    order = jnp.arange(page_slot.shape[1], dtype=jnp.int32)[None, :]
    held = (page_slot // PAGES_DEV == me) & (order < node_pages[:, None])
    row_of = jnp.max(jnp.where(held, page_slot % PAGES_DEV, -1), axis=1)
    target = shifted(me, dy, dz, dx, dc)
    leaf_t = request_leaf[target]
    mid_t = leaf_parent[leaf_t]
    send_row = jnp.maximum(jnp.maximum(row_of[0], row_of[1 + mid_t]), jnp.maximum(row_of[17 + leaf_t], 0))
    leaf = request_leaf[me]
    mid = leaf_parent[leaf]
    nodes = jnp.stack([jnp.zeros_like(mid), 1 + mid, 17 + leaf])
    counts = node_pages[nodes]
    first = jnp.cumsum(counts) - counts
    rows = page_slot[nodes]
    seen = jnp.clip(prefix_len[me] - PAGE * (first[:, None] + order), 0, PAGE)
    seen = jnp.where(order < counts[:, None], seen, 0)
    holder = shifted(me, -dy, -dz, -dx, -dc)
    match = (rows // PAGES_DEV).reshape(-1)[:, None] == holder[None, :]
    seen_slot = jnp.sum(jnp.where(match, seen.reshape(-1)[:, None], 0), axis=0)
    return send_row, seen_slot


def exchange(rows_ref, pk_ref, pv_ref, sk_ref, sv_ref, buf, other, send, sems, send_sem, recv_sem, fwd_send, fwd_recv, suf_send, suf_recv, near):
    me = lax.axis_index("store")
    p = lax.axis_index("pair")
    barrier = pltpu.get_barrier_semaphore()
    plane = [(dy, dx, dc) for dy in range(2) for dx in range(4) for dc in range(2) if (dy, dx, dc) != (0, 0, 0)]
    for dz in range(1, 8):
        pl.semaphore_signal(barrier, inc=1, device_id=(shifted(me, 0, dz, 0, 0), p), device_id_type=MESH)
    for dy, dx, dc in plane:
        pl.semaphore_signal(barrier, inc=1, device_id=(shifted(me, dy, 0, dx, dc), (p + dy) % 2), device_id_type=MESH)
    pl.semaphore_signal(barrier, inc=1, device_id=(me, 1 - p), device_id_type=MESH)

    def pack(page_ref):
        def body(d, _):
            page = page_ref[rows_ref[d]]
            start = pl.multiple_of(d * ROWS, ROWS)
            send[pl.ds(start, ROWS), :] = jnp.concatenate([page[:, :LANES], page[:, LANES:]], axis=0)
            return 0
        lax.fori_loop(0, SLOTS, body, 0)

    @pl.when(p == 0)
    def _():
        pack(pk_ref)

    @pl.when(p == 1)
    def _():
        pack(pv_ref)

    pl.semaphore_wait(barrier, 8 + len(plane))
    for dy, dx, dc in plane:
        pl.semaphore_signal(near, inc=1, device_id=(shifted(me, dy, 0, dx, dc), (p + dy) % 2), device_id_type=MESH)
    pl.semaphore_wait(near, len(plane))

    def suffix(i, ref):
        return pltpu.make_async_remote_copy(ref, other.at[i], suf_send.at[i], suf_recv.at[i], device_id=(me, 1 - p), device_id_type=MESH)

    suffix(0, sk_ref).start()
    suffix(1, sv_ref).start()
    self_copy = pltpu.make_async_copy(send.at[pl.ds(14 * ROWS, ROWS)], buf.at[p, pl.ds(14 * ROWS, ROWS)], sems)
    self_copy.start()

    def send_chunk(g, _):
        dy, dx = g // 4, g % 4
        for iz, dz in enumerate(Z_ORDER):
            for dc in range(2):
                start = pl.multiple_of(g * PER_CHUNK * ROWS, PER_CHUNK * ROWS) + (iz * 2 + dc) * ROWS
                start = pl.multiple_of(start, ROWS)
                copy = pltpu.make_async_remote_copy(
                    send.at[pl.ds(start, ROWS)], buf.at[p, pl.ds(start, ROWS)], send_sem, recv_sem.at[g],
                    device_id=(shifted(me, dy, dz, dx, dc), (p + dy) % 2), device_id_type=MESH)
                if dz == 0 and dc == 0:
                    pl.when(g != 0)(copy.start)
                else:
                    copy.start()
        return 0

    lax.fori_loop(0, CHUNKS, send_chunk, 0)

    def chunk_rows(g):
        return pl.ds(pl.multiple_of(g * PER_CHUNK * ROWS, PER_CHUNK * ROWS), PER_CHUNK * ROWS)

    def forward(g):
        q = (p + g // 4) % 2
        return pltpu.make_async_remote_copy(buf.at[q, chunk_rows(g)], buf.at[q, chunk_rows(g)], fwd_send.at[g], fwd_recv.at[g],
                                            device_id=(me, 1 - p), device_id_type=MESH)

    def arrived(n, sem):
        part = send.at[pl.ds(0, n * ROWS)]
        pltpu.make_async_copy(part, part, sem).wait()

    def pass_on(g, _):
        @pl.when(g == 0)
        def _():
            arrived(PER_CHUNK - 1, recv_sem.at[0])
            self_copy.wait()

        @pl.when(g != 0)
        def _():
            arrived(PER_CHUNK, recv_sem.at[g])
        forward(g).start()
        return 0

    lax.fori_loop(0, CHUNKS, pass_on, 0)

    def finish(g, _):
        forward(g).wait_send()
        arrived(PER_CHUNK, fwd_recv.at[g])
        return 0

    lax.fori_loop(0, CHUNKS, finish, 0)
    suffix(0, sk_ref).wait()
    suffix(1, sv_ref).wait()
    arrived(SLOTS - 1, send_sem)


def attend_block(state, head_queries, block_keys, block_values, allowed, score_scale):
    running_max, running_sum, weighted = state
    scores = jnp.einsum("hqd,khd->hqk", head_queries, block_keys, preferred_element_type=jnp.float32) * score_scale
    scores = jnp.where(allowed, scores, -1e30)
    new_max = jnp.maximum(running_max, jnp.max(scores, axis=-1))
    factor = jnp.exp(running_max - new_max)
    weights = jnp.exp(scores - new_max[..., None])
    running_sum = running_sum * factor + jnp.sum(weights, axis=-1)
    weighted = weighted * factor[..., None] + jnp.einsum(
        "hqk,khd->hqd", weights.astype(jnp.bfloat16), block_values, preferred_element_type=jnp.float32)
    return new_max, running_sum, weighted


def mirror_pos(pair_index):
    block_ids = jnp.stack([pair_index, 3 - pair_index])
    return (block_ids[:, None] * 128 + jnp.arange(128, dtype=jnp.int32)[None, :]).reshape(-1)


def local(queries, suffix_keys, suffix_values, page_keys, page_values, leaf_parent, node_pages, page_slot, request_leaf, prefix_len):
    me = lax.axis_index("store")
    p = lax.axis_index("pair")
    send_row, seen_slot = tables(leaf_parent, node_pages, page_slot, request_leaf, prefix_len, me)
    sk = suffix_keys.reshape(256, KVH * HD)
    sv = suffix_values.reshape(256, KVH * HD)
    vmem = pl.BlockSpec(memory_space=pltpu.VMEM)
    buf, other = pl.pallas_call(
        exchange,
        out_shape=(jax.ShapeDtypeStruct((2, SLOTS * ROWS, LANES), jnp.bfloat16), jax.ShapeDtypeStruct((2, 256, 1024), jnp.bfloat16)),
        in_specs=[pl.BlockSpec(memory_space=pltpu.SMEM)] + [vmem] * 4,
        out_specs=(vmem, vmem),
        scratch_shapes=[pltpu.VMEM((SLOTS * ROWS, LANES), jnp.bfloat16), pltpu.SemaphoreType.DMA, pltpu.SemaphoreType.DMA,
                        pltpu.SemaphoreType.DMA((CHUNKS,)), pltpu.SemaphoreType.DMA((CHUNKS,)), pltpu.SemaphoreType.DMA((CHUNKS,)),
                        pltpu.SemaphoreType.DMA((2,)), pltpu.SemaphoreType.DMA((2,)), pltpu.SemaphoreType.REGULAR],
        compiler_params=pltpu.CompilerParams(collective_id=1, has_side_effects=True, vmem_limit_bytes=48 * 2**20),
    )(send_row, page_keys, page_values, sk, sv)
    pages = buf.reshape(2, SLOTS, 2, PAGE, 4, HD).transpose(0, 1, 3, 2, 4, 5).reshape(2, SLOTS * PAGE, KVH, HD)
    usable = (jnp.arange(PAGE, dtype=jnp.int32)[None, :] < seen_slot[:, None]).reshape(1, 1, -1)
    scale = HD ** -0.5
    q = jnp.transpose(queries.reshape(256, KVH, GROUP, HD), (1, 0, 2, 3)).reshape(KVH, 256 * GROUP, HD)
    state = (jnp.full((KVH, 2048), -1e30, jnp.float32), jnp.zeros((KVH, 2048), jnp.float32), jnp.zeros((KVH, 2048, HD), jnp.float32))
    qp, op = mirror_pos(p), mirror_pos(1 - p)
    own = jnp.repeat(qp[:, None] >= qp[None, :], GROUP, axis=0)[None]
    theirs = jnp.repeat(qp[:, None] >= op[None, :], GROUP, axis=0)[None]
    state = attend_block(state, q, sk.reshape(-1, KVH, HD), sv.reshape(-1, KVH, HD), own, scale)
    state = attend_block(state, q, other[0].reshape(-1, KVH, HD), other[1].reshape(-1, KVH, HD), theirs, scale)
    for b in range(4):
        s = slice(b * 256, b * 256 + 256)
        state = attend_block(state, q, pages[0, s], pages[1, s], usable[:, :, s], scale)
    _, total, weighted = state
    result = (weighted / total[..., None]).reshape(KVH, 256, GROUP, HD)
    return jnp.transpose(result, (1, 0, 2, 3)).astype(jnp.bfloat16).reshape(queries.shape)


def solution(mesh):
    big = P("store", "pair", None, None, None)
    return jax.shard_map(
        local, mesh=mesh,
        in_specs=(big, big, big, P("store", None, None), P("store", None, None), P(), P(), P(), P(), P()),
        out_specs=big, check_vma=False)
```

time: 404 us -> 330 us (0.82)
  local copies, waits for them, and re-layouts: 139 us -> 39.8 us
  Pallas kernels: 0 us -> 84.7 us
  waiting for transfers between devices: 27.9 us -> 0 us
  starting transfers between devices: 27.3 us -> 0 us
  other arithmetic: 74.3 us -> 59.3 us
  matrix products: 129 us -> 138 us
    gather x6 -> x7, local copies, waits for them, and re-layouts: 99.2 us -> 7.57 us  [the longest x1 1.59 us: tables(): mid_t = leaf_parent[leaf_t]]
    pallas_call x0 -> x1, Pallas kernels: none -> 84.7 us  [local(): pl.pallas_call(exchange, out_shape=(jax.ShapeDtypeStruct((2, SLOTS * ROWS...]
    all_to_all x2 -> x0, waiting for transfers between devices: 27.9 us -> none  [the longest x1 21.8 us: local(): lax.all_to_all(sent_values, 'store', split_axis=0, concat_axis=0, tiled=T...]
    all_to_all x2 -> x0, starting transfers between devices: 25.1 us -> none  [the longest x1 16.8 us: local(): lax.all_to_all(sent_keys, 'store', split_axis=0, concat_axis=0, tiled=True)]
    dot_general x6, matrix products: 75.8 us -> 84.4 us  [attend_block(): jnp.einsum('hqk,khd->hqd', weights.astype(jnp.bfloat16), block_values, pr...]
    convert_element_type x3 -> x0, other arithmetic: 7.24 us -> none  [the longest x1 6.95 us: local(): jnp.transpose(result, (1, 0, 2, 3)).astype(jnp.bfloat16)]
    unnamed x28 -> x31, local copies, waits for them, and re-layouts: 17.4 us -> 11.5 us
    reshape x2 -> x0, local copies, waits for them, and re-layouts: 5.11 us -> none  [the longest x1 5.04 us: local(): queries.reshape(query_count, KVH, group_size, HD)]
  transfers between devices with their start and end apart: 4 -> 0, of which waited for: 2 -> 0; matrix products, arithmetic and copies ran while one was open for 48% -> 0% of each run, Pallas kernels for 0% -> 0%
where the time goes in v1:
time: 330 us; the launch traced here: 326 us
  matrix products  138 us (42%)
  Pallas kernels  84.7 us (26%)
  other arithmetic  59.3 us (18%)
  local copies, waits for them, and re-layouts  39.8 us (12%)
  between operations  4 us (1%)
    pallas_call x1, Pallas kernels, local(): pl.pallas_call(exchange, out_shape=(jax.ShapeDtypeStruct((2, SLOTS * ROWS...  84.7 us
    dot_general x6, matrix products, attend_block(): jnp.einsum('hqk,khd->hqd', weights.astype(jnp.bfloat16), block_values, pr...  84.4 us
    reduce_sum x6, other arithmetic, attend_block(): running_sum = running_sum * factor + jnp.sum(weights, axis=-1)  55.9 us
    dot_general x6, matrix products, attend_block(): jnp.einsum('hqd,khd->hqk', head_queries, block_keys, preferred_element_ty...  53.9 us
    unnamed x31, local copies, waits for them, and re-layouts  11.5 us
    reshape x1, local copies, waits for them, and re-layouts, local(): jnp.transpose(result, (1, 0, 2, 3)).astype(jnp.bfloat16)  7.27 us

profile of v1, /device:TPU:1, one launch (start us, length us, event | category | flops | bytes accessed | tf_op | source)
XLA Modules:
  0.0 326.1 jit_solution(14627347497384769922)
XLA Ops:
  12.2 5.4 %copy.64 = bf16[32,8,64,128]{3,2,1,0:T(8,128)(2,1)} copy(bf16[32,8,64,128]{3,1,2,0:T(8,128)(2,1)} %bitcast.217) | data formatting | bytes 8388608
  21.5 1.6 gather_fusion.1
  29.0 84.7 %shard_map.109 = (bf16[2,2048,512]{2,1,0:T(8,128)(2,1)}, bf16[2,256,1024]{2,1,0:T(8,128)(2,1)S(1)}) custom-call(s32[128]{0:T(128)S(1)} %maximum_maximum_fusion.rows_ref, bf16[64,8,1024]{2,1,0:T(8,128)(2,1)S(1)} %copy-done.4, bf16[64,8,1024]{2,1,0:T(8,128)(2,1)S(1)} %copy-done.5, bf16[256,1024]{1,0:T(8,128)(2,1)S(1)} %bitcast.196, bf16[256,1024]{1,0:T(8,128)(2,1)S(1)} %bitcast.198), custom_call_target="tpu_custom_call" | custom-call | tf_op jit(solution)/shard_map/pallas_call | solution.py:178
  113.6 3.3 copy.52
  116.9 11.3 %bitcast_reduce_fusion = (f32[8,2048]{1,0:T(8,128)S(1)}, f32[8,256,2048]{2,1,0:T(8,128)}) fusion(pred[256]{0:T(512)(128)(4,1)S(1)} %get-tuple-element.9, bf16[8,256,8,128]{3,2,0,1:T(8,128)(2,1)} %bitcast.201, bf16[2,1024,8,128]{3,1,2,0:T(8,128)(2,1)S(1)} %bitcast.209), kind=kOutput, calls=%fused_computation.7 | convolution fusion | flops 1086308352 | bytes 21561856 | tf_op jit(solution)/shard_map/hqd,khd->hqk/dot_general | solution.py:155
  128.2 7.2 %bitcast_reduce_fusion.1 = (f32[8,2048]{1,0:T(8,128)S(1)}, f32[8,256,2048]{2,1,0:T(8,128)}) fusion(pred[256]{0:T(512)(128)(4,1)S(1)} %get-tuple-element.10, bf16[8,256,8,128]{3,2,0,1:T(8,128)(2,1)S(1)} %bitcast.204, bf16[2,1024,8,128]{3,1,2,0:T(8,128)(2,1)S(1)} %bitcast.210), kind=kOutput, calls=%fused_computation.10 | convolution fusion | flops 1086308352 | bytes 21561856 | tf_op jit(solution)/shard_map/hqd,khd->hqk/dot_general | solution.py:155
  135.5 7.2 %bitcast_reduce_fusion.2 = (f32[8,2048]{1,0:T(8,128)S(1)}, f32[8,256,2048]{2,1,0:T(8,128)}) fusion(pred[256]{0:T(512)(128)(4,1)S(1)} %get-tuple-element.11, bf16[8,256,8,128]{3,2,0,1:T(8,128)(2,1)S(1)} %bitcast.205, bf16[2,1024,8,128]{3,1,2,0:T(8,128)(2,1)S(1)} %bitcast.211), kind=kOutput, calls=%fused_computation.13 | convolution fusion | flops 1086308352 | bytes 21561856 | tf_op jit(solution)/shard_map/hqd,khd->hqk/dot_general | solution.py:155
  142.7 7.2 %bitcast_reduce_fusion.3 = (f32[8,2048]{1,0:T(8,128)S(1)}, f32[8,256,2048]{2,1,0:T(8,128)}) fusion(pred[256]{0:T(512)(128)(4,1)S(1)} %get-tuple-element.12, bf16[8,256,8,128]{3,2,0,1:T(8,128)(2,1)S(1)} %bitcast.206, bf16[2,1024,8,128]{3,1,2,0:T(8,128)(2,1)S(1)} %bitcast.212), kind=kOutput, calls=%fused_computation.16 | convolution fusion | flops 1086308352 | bytes 21561856 | tf_op jit(solution)/shard_map/hqd,khd->hqk/dot_general | solution.py:155
  152.2 10.2 %fusion.9 = (f32[8,2048]{1,0:T(8,128)S(1)}, f32[8,256,2048]{2,1,0:T(8,128)}) fusion(pred[2048,256]{0,1:T(8,128)(4,1)S(1)} %copy.47, bf16[8,256,8,128]{3,2,0,1:T(8,128)(2,1)} %bitcast.202, bf16[256,8,128]{2,1,0:T(8,128)(2,1)S(1)} %bitcast.219), kind=kOutput, calls=%fused_computation.31 | convolution fusion | flops 1086308352 | bytes 22085632 | tf_op jit(solution)/shard_map/hqd,khd->hqk/dot_general | solution.py:155
  163.6 10.7 %fusion.4 = (f32[8,2048]{1,0:T(8,128)S(1)}, f32[8,2048,256]{1,2,0:T(8,128)}) fusion(pred[2048,256]{0,1:T(8,128)(4,1)S(1)} %copy.42, bf16[256,8,128]{2,1,0:T(8,128)(2,1)S(1)} %bitcast.221, bf16[8,256,8,128]{3,2,0,1:T(8,128)(2,1)} %bitcast.203), kind=kOutput, calls=%fused_computation.26 | convolution fusion | flops 1086308352 | bytes 22085632 | tf_op jit(solution)/shard_map/hqd,khd->hqk/dot_general | solution.py:155
  174.3 9.3 %fusion.16 = f32[8,2048]{1,0:T(8,128)S(1)} fusion(f32[8,256,2048]{2,1,0:T(8,128)} %get-tuple-element.33, f32[8,2048]{1,0:T(8,128)S(1)} %get-tuple-element.19, pred[256]{0:T(512)(128)(4,1)S(1)} %get-tuple-element.9), kind=kLoop, calls=%fused_computation.38 | loop fusion | flops 16760832 | bytes 16908544 | tf_op jit(solution)/shard_map/reduce_sum | solution.py:160
  183.6 9.3 %fusion.14 = f32[8,2048]{1,0:T(8,128)S(1)} fusion(f32[8,256,2048]{2,1,0:T(8,128)} %get-tuple-element.35, f32[8,2048]{1,0:T(8,128)S(1)} %get-tuple-element.20, pred[256]{0:T(512)(128)(4,1)S(1)} %get-tuple-element.10), kind=kLoop, calls=%fused_computation.36 | loop fusion | flops 16760832 | bytes 16908544 | tf_op jit(solution)/shard_map/reduce_sum | solution.py:160
  192.9 9.3 %fusion.12 = f32[8,2048]{1,0:T(8,128)S(1)} fusion(f32[8,256,2048]{2,1,0:T(8,128)} %get-tuple-element.37, f32[8,2048]{1,0:T(8,128)S(1)} %get-tuple-element.21, pred[256]{0:T(512)(128)(4,1)S(1)} %get-tuple-element.11), kind=kLoop, calls=%fused_computation.34 | loop fusion | flops 16760832 | bytes 16908544 | tf_op jit(solution)/shard_map/reduce_sum | solution.py:160
  202.1 9.4 %fusion.10 = f32[8,2048]{1,0:T(8,128)S(1)} fusion(f32[8,256,2048]{2,1,0:T(8,128)} %get-tuple-element.39, f32[8,2048]{1,0:T(8,128)S(1)} %get-tuple-element.22, pred[256]{0:T(512)(128)(4,1)S(1)} %get-tuple-element.12), kind=kLoop, calls=%fused_computation.32 | loop fusion | flops 16760832 | bytes 16908544 | tf_op jit(solution)/shard_map/reduce_sum | solution.py:160
  211.6 9.3 %fusion.5 = f32[8,2048]{1,0:T(8,128)S(1)} fusion(f32[8,256,2048]{2,1,0:T(8,128)} %get-tuple-element.41, f32[8,2048]{1,0:T(8,128)S(1)} %get-tuple-element.23, pred[2048,256]{0,1:T(8,128)(4,1)S(1)} %copy.47), kind=kLoop, calls=%fused_computation.27 | loop fusion | flops 16760832 | bytes 17432576 | tf_op jit(solution)/shard_map/reduce_sum | solution.py:160
  220.9 9.3 %fusion.7 = f32[8,2048]{1,0:T(8,128)S(1)} fusion(f32[8,2048,256]{1,2,0:T(8,128)} %get-tuple-element.43, f32[8,2048]{1,0:T(8,128)S(1)} %get-tuple-element.27, pred[2048,256]{0,1:T(8,128)(4,1)S(1)} %copy.42), kind=kLoop, calls=%fused_computation.29 | loop fusion | flops 16760832 | bytes 17432576 | tf_op jit(solution)/shard_map/reduce_sum | solution.py:160
  230.4 13.8 %fusion.20 = f32[8,2048,128]{2,1,0:T(8,128)} fusion(f32[8,256,2048]{2,1,0:T(8,128)} %get-tuple-element.35, f32[8,2048]{1,0:T(8,128)S(1)} %get-tuple-element.20, pred[256]{0:T(512)(128)(4,1)S(1)} %get-tuple-element.10, bf16[2,1024,8,128]{3,1,2,0:T(8,128)(2,1)} %bitcast.213), kind=kOutput, calls=%fused_computation.41 | convolution fusion | flops 1090519040 | bytes 25755904 | tf_op jit(solution)/shard_map/hqk,khd->hqd/dot_general | solution.py:161
  244.1 13.5 %fusion.22 = f32[8,2048,128]{2,1,0:T(8,128)} fusion(f32[8,256,2048]{2,1,0:T(8,128)} %get-tuple-element.37, f32[8,2048]{1,0:T(8,128)S(1)} %get-tuple-element.21, pred[256]{0:T(512)(128)(4,1)S(1)} %get-tuple-element.11, bf16[2,1024,8,128]{3,1,2,0:T(8,128)(2,1)} %bitcast.214), kind=kOutput, calls=%fused_computation.42 | convolution fusion | flops 1090519040 | bytes 25755904 | tf_op jit(solution)/shard_map/hqk,khd->hqd/dot_general | solution.py:161
  257.6 13.5 %fusion.24 = f32[8,2048,128]{2,1,0:T(8,128)} fusion(f32[8,256,2048]{2,1,0:T(8,128)} %get-tuple-element.39, f32[8,2048]{1,0:T(8,128)S(1)} %get-tuple-element.22, pred[256]{0:T(512)(128)(4,1)S(1)} %get-tuple-element.12, bf16[2,1024,8,128]{3,1,2,0:T(8,128)(2,1)} %bitcast.215), kind=kOutput, calls=%fused_computation.43 | convolution fusion | flops 1090519040 | bytes 25755904 | tf_op jit(solution)/shard_map/hqk,khd->hqd/dot_general | solution.py:161
  271.5 10.5 %fusion.28 = f32[8,2048,128]{2,1,0:T(8,128)} fusion(f32[8,256,2048]{2,1,0:T(8,128)} %get-tuple-element.41, f32[8,2048]{1,0:T(8,128)S(1)} %get-tuple-element.23, pred[2048,256]{0,1:T(8,128)(4,1)S(1)} %copy.47, bf16[256,8,128]{2,1,0:T(8,128)(2,1)S(1)} %bitcast.220), kind=kOutput, calls=%fused_computation.45 | convolution fusion | flops 1090519040 | bytes 26279936 | tf_op jit(solution)/shard_map/hqk,khd->hqd/dot_general | solution.py:161
  282.1 10.5 %fusion.26 = f32[8,2048,128]{2,1,0:T(8,128)} fusion(f32[8,2048,256]{1,2,0:T(8,128)} %get-tuple-element.43, f32[8,2048]{1,0:T(8,128)S(1)} %get-tuple-element.27, pred[2048,256]{0,1:T(8,128)(4,1)S(1)} %copy.42, bf16[256,8,128]{2,1,0:T(8,128)(2,1)S(1)} %bitcast.222), kind=kOutput, calls=%fused_computation.44 | convolution fusion | flops 1090519040 | bytes 26279936 | tf_op jit(solution)/shard_map/hqk,khd->hqd/dot_general | solution.py:161
  292.7 22.6 %fusion.66 = bf16[256,8,8,128]{3,2,0,1:T(8,128)(2,1)S(1)} fusion(f32[8,2048]{1,0:T(8,128)S(1)} %get-tuple-element.13, f32[8,2048]{1,0:T(8,128)S(1)} %get-tuple-element.18, f32[8,2048,128]{2,1,0:T(8,128)} %fusion.20, f32[8,2048]{1,0:T(8,128)S(1)} %get-tuple-element.17, f32[8,2048,128]{2,1,0:T(8,128)} %fusion.22, f32[8,2048]{1,0:T(8,128)S(1)} %get-tuple-element.16, ...), kind=kOutput, calls=%fused_computation.83 | convolution fusion | flops 1117782016 | bytes 63963392 | tf_op jit(solution)/shard_map/hqk,khd->hqd/dot_general | solution.py:161
  315.3 3.1 copy.57
  318.4 7.3 %reshape.934 = bf16[1,1,2,128,8192]{4,3,2,1,0:T(8,128)(2,1)} reshape(bf16[256,8,8,128]{3,2,1,0:T(8,128)(2,1)} %copy.57) | data formatting | bytes 8388608 | tf_op jit(solution)/shard_map/reshape | solution.py:203
  (80 shorter events, 22.6 us)
Async XLA Ops:
  24.4 1.0 copy-start
  25.5 1.0 copy-start.2
  26.5 1.2 copy-start.4
  27.7 1.2 copy-start.5
  29.0 99.3 %copy-start.6 = (bf16[32,8,64,128]{3,2,1,0:T(8,128)(2,1)S(1)}, bf16[32,8,64,128]{3,2,1,0:T(8,128)(2,1)}, u32[]{:S(2)}) copy-start(bf16[32,8,64,128]{3,2,1,0:T(8,128)(2,1)} %copy.64) | copy-start | bytes 12582916
  116.9 25.7 %copy-start.7 = (bf16[2,128,8,2,4,128]{5,2,1,4,3,0:T(8,128)(2,1)}, bf16[2,128,8,2,4,128]{5,2,1,4,3,0:T(8,128)(2,1)S(1)}, u32[]{:S(2)}) copy-start(bf16[2,128,8,2,4,128]{5,2,1,4,3,0:T(8,128)(2,1)S(1)} %copy.52) | copy-start | bytes 12582916
  149.9 13.6 %copy-start.1 = (bf16[1,1,2,128,1024]{4,3,2,1,0:T(8,128)(2,1)S(1)}, bf16[1,1,2,128,1024]{4,3,2,1,0:T(8,128)(2,1)}, u32[]{:S(2)}) copy-start(bf16[1,1,2,128,1024]{4,3,2,1,0:T(8,128)(2,1)} %param.12) | copy-start | bytes 1572868
  271.1 10.9 %copy-start.3 = (bf16[1,1,2,128,1024]{4,3,2,1,0:T(8,128)(2,1)S(1)}, bf16[1,1,2,128,1024]{4,3,2,1,0:T(8,128)(2,1)}, u32[]{:S(2)}) copy-start(bf16[1,1,2,128,1024]{4,3,2,1,0:T(8,128)(2,1)} %param.13) | copy-start | bytes 1572868
  271.5 21.2 %slice-start = ((s8[16777216]{0:T(1024)(128)(4,1)}), s8[4194304]{0:T(1024)(128)(4,1)S(1)}, s32[]{:S(2)}) async-start(s8[16777216]{0:T(1024)(128)(4,1)} %bitcast.207), calls=%async_computation | async-start | bytes 8388608
  271.5 21.2 %slice-start.1 = ((s8[16777216]{0:T(1024)(128)(4,1)}), s8[4194304]{0:T(1024)(128)(4,1)S(1)}, s32[]{:S(2)}) async-start(s8[16777216]{0:T(1024)(128)(4,1)} %bitcast.207), calls=%async_computation.1 | async-start | bytes 8388608
  282.0 10.6 %slice-start.2 = ((s8[16777216]{0:T(1024)(128)(4,1)}), s8[4194304]{0:T(1024)(128)(4,1)S(1)}, s32[]{:S(2)}) async-start(s8[16777216]{0:T(1024)(128)(4,1)} %bitcast.207), calls=%async_computation.2 | async-start | bytes 8388608
  282.1 10.5 %slice-start.3 = ((s8[16777216]{0:T(1024)(128)(4,1)}), s8[4194304]{0:T(1024)(128)(4,1)S(1)}, s32[]{:S(2)}) async-start(s8[16777216]{0:T(1024)(128)(4,1)} %bitcast.207), calls=%async_computation.3 | async-start | bytes 8388608

commit v2 on v1

v2 whole, which is shorter than its diff:
```python
import jax
import jax.numpy as jnp
from jax import lax
from jax.experimental import pallas as pl
from jax.experimental.pallas import tpu as pltpu
from jax.sharding import PartitionSpec as P

QH = 64
KVH = 8
HD = 128
GROUP = QH // KVH
BLK = 128
LOCAL = 2 * BLK
PAGE = 8
PAGES_DEV = 64
MIDS = 16
SLOTS = 128
CHUNKS = 8
PER_CHUNK = SLOTS // CHUNKS
CHUNK_KEYS = PER_CHUNK * PAGE
ROWS = 16
LANES = 512
CHUNK_ROWS = PER_CHUNK * ROWS
STEP_KEYS = 256
DIRECT = (6, 7)
FIRST_DIRECT = DIRECT[0]
Z_ORDER = (1, 0, 2, 7, 3, 6, 4, 5)
SELF_ITEM = 2
SCALE = HD ** -0.5 * 1.4426950408889634
HIDDEN = -1e30
MESH = pl.DeviceIdType.MESH


def shifted(me, dy, dz, dx, dc):
    yh, z, x, c = me // 64, me // 8 % 8, me // 2 % 4, me % 2
    return (((yh + dy) % 2 * 8 + (z + dz) % 8) * 4 + (x + dx) % 4) * 2 + (c + dc) % 2


def chunk_step(g):
    return g % 2, g // 2


def score(q, keys):
    return lax.dot_general(q, keys, (((1,), (1,)), ((), ())), preferred_element_type=jnp.float32)


def load(h, rows, state):
    return tuple(ref[h, rows] for ref in state)


def attend(scores, values, before, bias=None, causal=False):
    scores = scores * SCALE
    if bias is not None:
        scores = scores + bias
    if causal:
        shape = scores.shape
        ordered = lax.broadcasted_iota(jnp.int32, shape, 0) >= lax.broadcasted_iota(jnp.int32, shape, 1)
        scores = jnp.where(ordered, scores, HIDDEN)
    top = jnp.max(scores, axis=1, keepdims=True)
    if before is None:
        new_max = jnp.broadcast_to(top, (scores.shape[0], HD))
    else:
        old_out, old_max, old_total = before
        new_max = jnp.maximum(old_max, top)
        factor = jnp.exp2(old_max - new_max)
    parts = [jnp.exp2(scores[:, j * 128:j * 128 + 128] - new_max) for j in range(scores.shape[1] // 128)]
    total = parts[0]
    for part in parts[1:]:
        total = total + part
    weights = [part.astype(jnp.bfloat16) for part in parts]
    weights = jnp.concatenate(weights, axis=1) if len(parts) > 1 else weights[0]
    out = jnp.dot(weights, values, preferred_element_type=jnp.float32)
    if before is not None:
        total = total + old_total * factor
        out = out + old_out * factor
    return out, new_max, total


def group_heads(k, q_ref, rows, keys, values, state, finish, first=False, **mask):
    scores, before = [None] * GROUP, [None] * GROUP
    for g in range(GROUP + AHEAD):
        if g < GROUP:
            h = k * GROUP + g
            scores[g] = score(q_ref[rows, head_columns(h)], keys)
            before[g] = None if first else load(h, rows, state)
        if g >= AHEAD:
            done = g - AHEAD
            finish(k * GROUP + done, attend(scores[done], values, before[done], **mask))


AHEAD = 8


def keep(h, rows, state, result):
    for ref, value in zip(state, result):
        ref[h, rows] = value


def head_columns(h):
    return pl.ds(pl.multiple_of(h * HD, HD), HD)


def suffix_own(q_ref, suf, state):
    rows = pl.ds(0, LOCAL)

    def body(k, _):
        keys, values = suf[0, :, head_columns(k)], suf[1, :, head_columns(k)]
        group_heads(k, q_ref, rows, keys, values, state, lambda h, r: keep(h, rows, state, r), first=True, causal=True)
        return 0
    lax.fori_loop(0, KVH, body, 0)


def suffix_other(q_ref, other, state, p):
    def run(rows, key_count):
        def body(k, _):
            keys, values = other[0, pl.ds(0, key_count), head_columns(k)], other[1, pl.ds(0, key_count), head_columns(k)]
            group_heads(k, q_ref, rows, keys, values, state, lambda h, r: keep(h, rows, state, r))
            return 0
        lax.fori_loop(0, KVH, body, 0)

    @pl.when(p == 0)
    def _():
        run(pl.ds(BLK, BLK), LOCAL)

    @pl.when(p == 1)
    def _():
        run(pl.ds(0, LOCAL), BLK)


def prefix_step(s, q_ref, paged, bias_ref, state):
    rows, span = pl.ds(0, LOCAL), pl.ds(s * STEP_KEYS, STEP_KEYS)

    def body(k, _):
        group_heads(k, q_ref, rows, paged[0, k, span], paged[1, k, span], state,
                    lambda h, r: keep(h, rows, state, r), bias=bias_ref[pl.ds(0, 1), span])
        return 0
    lax.fori_loop(0, KVH, body, 0)


def last_step(s, q_ref, paged, bias_ref, state, out_ref, out_sem):
    rows, span = pl.ds(0, LOCAL), pl.ds(s * STEP_KEYS, STEP_KEYS)

    def out_copy(k):
        columns = pl.ds(pl.multiple_of(k * GROUP * HD, GROUP * HD), GROUP * HD)
        return pltpu.make_async_copy(q_ref.at[:, columns], out_ref.at[:, columns], out_sem.at[k])

    def divide(h, result):
        out, _, total = result
        total = jnp.sum(total, axis=1, keepdims=True)
        q_ref[:, head_columns(h)] = (out / total).astype(jnp.bfloat16)

    def body(k, _):
        group_heads(k, q_ref, rows, paged[0, k, span], paged[1, k, span], state, divide, bias=bias_ref[pl.ds(0, 1), span])
        out_copy(k).start()
        return 0
    lax.fori_loop(0, KVH, body, 0)

    def finish(k, _):
        out_copy(k).wait()
        return 0
    lax.fori_loop(0, KVH, finish, 0)


def unfold(g, land, paged):
    for i in range(2):
        for lane in range(4):
            block = land[i, pl.ds(g * CHUNK_ROWS, CHUNK_ROWS), lane * HD:(lane + 1) * HD]
            block = block.astype(jnp.float32).reshape(PER_CHUNK, 2, PAGE, HD)
            for half in range(2):
                part = block[:, half].reshape(CHUNK_KEYS, HD).astype(jnp.bfloat16)
                paged[i, half * 4 + lane, pl.ds(g * CHUNK_KEYS, CHUNK_KEYS)] = part


def visible_bias(me, parent_ref, pages_ref, leaf_ref, length_ref, slot_ref, bias_ref):
    leaf = leaf_ref[me]
    mid = parent_ref[leaf]
    length = length_ref[me]
    width = slot_ref.shape[1]
    key = lax.broadcasted_iota(jnp.int32, (1, SLOTS * PAGE), 1)
    d = key // PAGE
    g, item = d // PER_CHUNK, d % PER_CHUNK
    iz, dc = item // 2, item % 2
    dz = jnp.where(iz % 2 == 0, iz // 2 + 1, (8 - iz // 2) % 8)
    dy, dx = chunk_step(g)
    holder = shifted(me + jnp.zeros_like(key), 2 - dy, 8 - dz, 4 - dx, 2 - dc).astype(jnp.float32)
    across = lax.broadcasted_iota(jnp.int32, (width, width), 1)
    down = lax.broadcasted_iota(jnp.int32, (width, width), 0)
    order = lax.broadcasted_iota(jnp.int32, (width, 1), 0)
    seen = jnp.zeros(key.shape, jnp.float32)
    first = 0
    for node in (0, 1 + mid, 1 + MIDS + leaf):
        count = pages_ref[node]
        row = (slot_ref[pl.ds(node, 1), :] // PAGES_DEV).astype(jnp.float32)
        column = jnp.sum(jnp.where(across == down, jnp.broadcast_to(row, (width, width)), 0.0), axis=1, keepdims=True)
        tokens = jnp.clip(length - PAGE * (first + order), 0, PAGE)
        tokens = jnp.where(order < count, tokens, 0).astype(jnp.float32)
        match = column == holder
        seen = seen + jnp.sum(jnp.where(match, tokens, 0.0), axis=0, keepdims=True)
        first = first + count
    shown = (key % PAGE).astype(jnp.float32) < seen
    bias_ref[...] = jnp.broadcast_to(jnp.where(shown, 0.0, HIDDEN), bias_ref.shape)


def kernel(parent_ref, pages_ref, leaf_ref, length_ref, slot_ref, pk_ref, pv_ref, q_hbm, sk_hbm, sv_hbm, out_ref,
           q_ref, suf, other, land, send, paged, acc_ref, max_ref, sum_ref, bias_ref, row_vec, row_smem,
           load_sem, row_sem, self_sem, send_sem, recv_sem, fwd_send, fwd_recv, suf_send, suf_recv, out_sem, near):
    me = lax.axis_index("store")
    p = lax.axis_index("pair")
    state = (acc_ref, max_ref, sum_ref)
    barrier = pltpu.get_barrier_semaphore()
    plane = [(dy, dx, dc) for dy in range(2) for dx in range(4) for dc in range(2) if (dy, dx, dc) != (0, 0, 0)]

    def tell(sem, dy, dz, dx, dc):
        pl.semaphore_signal(sem, inc=1, device_id=(shifted(me, dy, dz, dx, dc), (p + dy) % 2), device_id_type=MESH)

    for dy, dx, dc in plane:
        tell(barrier, dy, 0, dx, dc)
    for dz in range(1, 8):
        tell(barrier, 0, dz, 0, 0)
    pl.semaphore_signal(barrier, inc=1, device_id=(me, 1 - p), device_id_type=MESH)

    loads = [pltpu.make_async_copy(sk_hbm, suf.at[0], load_sem.at[0]),
             pltpu.make_async_copy(sv_hbm, suf.at[1], load_sem.at[1]),
             pltpu.make_async_copy(q_hbm, q_ref, load_sem.at[2])]
    for copy in loads:
        copy.start()

    places = slot_ref[...]
    mine = jnp.where(places // PAGES_DEV == me, places % PAGES_DEV, 0)
    best = jnp.max(mine, axis=1, keepdims=True)
    row_vec[...] = jnp.broadcast_to(best, row_vec.shape)
    to_smem = pltpu.make_async_copy(row_vec, row_smem, row_sem)
    to_smem.start()
    to_smem.wait()

    def target(g, item):
        dy, dx = chunk_step(g)
        return dy, Z_ORDER[item // 2], dx, item % 2

    def pack(g, _):
        for item in range(PER_CHUNK):
            dy, dz, dx, dc = target(g, item)
            leaf = leaf_ref[shifted(me, dy, dz, dx, dc)]
            mid = parent_ref[leaf]
            row = jnp.maximum(jnp.maximum(row_smem[0, 0], row_smem[1 + mid, 0]), row_smem[1 + MIDS + leaf, 0])
            start = pl.multiple_of(g * CHUNK_ROWS + item * ROWS, ROWS)

            def put(i, page_ref):
                page = page_ref[jnp.clip(row, 0, PAGES_DEV - 1)]
                send[i, pl.ds(start, ROWS), :] = jnp.concatenate([page[:, :LANES], page[:, LANES:]], axis=0)

            @pl.when((p == 0) | (g >= FIRST_DIRECT))
            def _():
                put(0, pk_ref)

            @pl.when((p == 1) | (g >= FIRST_DIRECT))
            def _():
                put(1, pv_ref)
        return 0

    def chunk_span(g):
        return pl.ds(pl.multiple_of(g * CHUNK_ROWS, CHUNK_ROWS), CHUNK_ROWS)

    def own_item(g):
        span = pl.ds(SELF_ITEM * ROWS, ROWS)
        return pltpu.make_async_copy(send.at[p, span], land.at[p, span], self_sem)

    def send_chunk(g, i, extra=0):
        for item in range(PER_CHUNK):
            dy, dz, dx, dc = target(g, item)
            span = pl.ds(pl.multiple_of(g * CHUNK_ROWS + item * ROWS, ROWS), ROWS)
            copy = pltpu.make_async_remote_copy(
                send.at[i, span], land.at[i, span], send_sem.at[extra], recv_sem.at[g],
                device_id=(shifted(me, dy, dz, dx, dc), (p + dy) % 2), device_id_type=MESH)
            if item == SELF_ITEM:
                pl.when(g != 0)(copy.start)
            else:
                copy.start()

    lax.fori_loop(0, 2, pack, 0)
    pl.semaphore_wait(barrier, 8 + len(plane))
    for dy, dx, dc in plane:
        tell(near, dy, 0, dx, dc)
    loads[0].wait()
    loads[1].wait()

    def suffix_copy(i, rows):
        return pltpu.make_async_remote_copy(suf.at[i, pl.ds(0, rows)], other.at[i, pl.ds(0, rows)], suf_send.at[i], suf_recv.at[i],
                                            device_id=(me, 1 - p), device_id_type=MESH)

    for rows, who in ((BLK, 0), (LOCAL, 1)):
        @pl.when(p == who)
        def _():
            suffix_copy(0, rows).start()
            suffix_copy(1, rows).start()
    pl.semaphore_wait(near, len(plane))
    own_item(0).start()

    def pack_send(g, _):
        @pl.when(g >= 2)
        def _():
            pack(g, 0)

        send_chunk(g, p)

        @pl.when(g >= FIRST_DIRECT)
        def _():
            send_chunk(g, 1 - p, 1)
        return 0

    lax.fori_loop(0, CHUNKS, pack_send, 0)

    def forward(g):
        q = (p + g % 2) % 2
        part = land.at[q, chunk_span(g)]
        return pltpu.make_async_remote_copy(part, part, fwd_send.at[g], fwd_recv.at[g], device_id=(me, 1 - p), device_id_type=MESH)

    def arrived(items, sem):
        part = send.at[0, pl.ds(0, items * ROWS)]
        pltpu.make_async_copy(part, part, sem).wait()

    def receive(g):
        if g in DIRECT:
            arrived(2 * PER_CHUNK, recv_sem.at[g])
            return
        arrived(PER_CHUNK - (g == 0), recv_sem.at[g])
        if g == 0:
            own_item(0).wait()
        forward(g).start()

    def whole(g):
        if g not in DIRECT:
            arrived(PER_CHUNK, fwd_recv.at[g])
        unfold(g, land, paged)

    visible_bias(me, parent_ref, pages_ref, leaf_ref, length_ref, slot_ref, bias_ref)
    loads[2].wait()
    suffix_own(q_ref, suf, state)
    receive(0)
    receive(1)
    for rows, who in ((LOCAL, 0), (BLK, 1)):
        @pl.when(p == who)
        def _():
            for i in range(2):
                pltpu.make_async_copy(suf.at[i, pl.ds(0, rows)], suf.at[i, pl.ds(0, rows)], suf_recv.at[i]).wait()
    suffix_other(q_ref, other, state, p)
    receive(2)
    whole(0)
    receive(3)
    whole(1)
    prefix_step(0, q_ref, paged, bias_ref, state)
    receive(4)
    whole(2)
    receive(5)
    whole(3)
    prefix_step(1, q_ref, paged, bias_ref, state)
    whole(4)
    whole(5)
    prefix_step(2, q_ref, paged, bias_ref, state)
    receive(6)
    whole(6)
    receive(7)
    whole(7)
    last_step(3, q_ref, paged, bias_ref, state, out_ref, out_sem)

    for g in range(CHUNKS):
        if g not in DIRECT:
            forward(g).wait_send()
    for rows, who in ((BLK, 0), (LOCAL, 1)):
        @pl.when(p == who)
        def _():
            suffix_copy(0, rows).wait_send()
            suffix_copy(1, rows).wait_send()
    arrived(SLOTS - 1, send_sem.at[0])
    arrived(len(DIRECT) * PER_CHUNK, send_sem.at[1])


def local(queries, suffix_keys, suffix_values, page_keys, page_values, leaf_parent, node_pages, page_slot, request_leaf, prefix_len):
    vmem = pl.BlockSpec(memory_space=pltpu.VMEM)
    smem = pl.BlockSpec(memory_space=pltpu.SMEM)
    anywhere = pl.BlockSpec(memory_space=pl.ANY)
    bf16, f32 = jnp.bfloat16, jnp.float32
    dma = pltpu.SemaphoreType.DMA
    nodes = page_slot.shape[0]
    out = pl.pallas_call(
        kernel,
        out_shape=jax.ShapeDtypeStruct((LOCAL, QH * HD), bf16),
        in_specs=[smem] * 4 + [vmem] * 3 + [anywhere] * 3,
        out_specs=anywhere,
        scratch_shapes=[
            pltpu.VMEM((LOCAL, QH * HD), bf16),
            pltpu.VMEM((2, LOCAL, KVH * HD), bf16),
            pltpu.VMEM((2, LOCAL, KVH * HD), bf16),
            pltpu.VMEM((2, SLOTS * ROWS, LANES), bf16),
            pltpu.VMEM((2, SLOTS * ROWS, LANES), bf16),
            pltpu.VMEM((2, KVH, SLOTS * PAGE, HD), bf16),
            pltpu.VMEM((QH, LOCAL, HD), f32),
            pltpu.VMEM((QH, LOCAL, HD), f32),
            pltpu.VMEM((QH, LOCAL, HD), f32),
            pltpu.VMEM((8, SLOTS * PAGE), f32),
            pltpu.VMEM((nodes, 128), jnp.int32),
            pltpu.SMEM((nodes, 128), jnp.int32),
            dma((3,)), dma, dma, dma((2,)), dma((CHUNKS,)), dma((CHUNKS,)), dma((CHUNKS,)), dma((2,)), dma((2,)), dma((KVH,)),
            pltpu.SemaphoreType.REGULAR,
        ],
        compiler_params=pltpu.CompilerParams(collective_id=1, has_side_effects=True, vmem_limit_bytes=60 * 2**20),
    )(leaf_parent, node_pages, request_leaf, prefix_len, page_slot, page_keys, page_values,
      queries.reshape(LOCAL, QH * HD), suffix_keys.reshape(LOCAL, KVH * HD), suffix_values.reshape(LOCAL, KVH * HD))
    return out.reshape(queries.shape)


def solution(mesh):
    big = P("store", "pair", None, None, None)
    return jax.shard_map(
        local, mesh=mesh,
        in_specs=(big, big, big, P("store", None, None), P("store", None, None), P(), P(), P(), P(), P()),
        out_specs=big, check_vma=False)
```

time: 330 us -> 93.7 us (0.28); the launches traced: 326 us -> 93.4 us
  matrix products: 138 us -> 0 us
  other arithmetic: 59.3 us -> 0 us
  local copies, waits for them, and re-layouts: 39.8 us -> 6.11 us
  between operations: 4 us -> 0.01 us
    dot_general x12 -> x0, matrix products: 138 us -> none  [the longest x6 84.4 us: attend_block(): jnp.einsum('hqk,khd->hqd', weights.astype(jnp.bfloat16), block_values, pr...]
    reduce_sum x7 -> x0, other arithmetic: 56 us -> none  [the longest x6 55.9 us: attend_block(): running_sum = running_sum * factor + jnp.sum(weights, axis=-1)]
    gather x7 -> x0, local copies, waits for them, and re-layouts: 7.57 us -> none  [the longest x1 1.59 us: tables(): mid_t = leaf_parent[leaf_t]]
    reshape x1 -> x0, local copies, waits for them, and re-layouts: 7.27 us -> none  [local(): jnp.transpose(result, (1, 0, 2, 3)).astype(jnp.bfloat16)]
    unnamed x31 -> x2, local copies, waits for them, and re-layouts: 11.5 us -> 6.11 us
    dynamic_slice x3 -> x0, local copies, waits for them, and re-layouts: 3.72 us -> none  [the longest x1 1.24 us: tables(): mid = leaf_parent[leaf]]
where the time goes in v2:
time: 93.7 us; the launch traced here: 93.4 us
  Pallas kernels  87.3 us (93%)
  local copies, waits for them, and re-layouts  6.11 us (7%)
    pallas_call x1, Pallas kernels, local(): pl.pallas_call(kernel, out_shape=jax.ShapeDtypeStruct((LOCAL, QH * HD), b...  87.3 us
    unnamed x2, local copies, waits for them, and re-layouts  6.11 us

profile of v2, /device:TPU:1, one launch (start us, length us, event | category | flops | bytes accessed | tf_op | source)
XLA Modules:
  0.0 93.4 jit_solution(5961525660196828236)
XLA Ops:
  0.0 1.5 %copy.11.slot_ref = s32[81,64]{1,0:T(8,128)} copy(s32[81,64]{0,1:T(8,128)} %param.17) | data formatting | bytes 41472 | tf_op args[7]
  1.5 87.3 %shard_map.100 = bf16[256,8192]{1,0:T(8,128)(2,1)} custom-call(s32[64]{0:T(128)} %parent_ref.1, s32[81]{0:T(128)} %pages_ref.1, s32[128]{0:T(128)} %leaf_ref.1, s32[128]{0:T(128)} %length_ref.1, s32[81,64]{1,0:T(8,128)} %copy.11.slot_ref, bf16[64,8,1024]{2,1,0:T(8,128)(2,1)} %pk_ref.1, bf16[64,8,1024]{2,1,0:T(8,128)(2,1)} %pv_ref.1, ...), custom_call_target="tpu_custom_call" | custom-call | tf_op jit(solution)/shard_map/pallas_call | solution.py:385
  88.8 4.6 %copy.13 = bf16[1,1,2,128,8192]{4,3,2,1,0:T(8,128)(2,1)} copy(bf16[1,1,2,128,8192]{4,3,2,1,0:T(8,128)(2,1)} %bitcast.4) | data formatting | bytes 8388608

commit v3 on v2

--- a/solution.py
+++ b/solution.py
@@ -21,7 +21,6 @@
 ROWS = 16
 LANES = 512
 CHUNK_ROWS = PER_CHUNK * ROWS
-STEP_KEYS = 256
 DIRECT = (6, 7)
 FIRST_DIRECT = DIRECT[0]
 Z_ORDER = (1, 0, 2, 7, 3, 6, 4, 5)
@@ -127,8 +126,8 @@
         run(pl.ds(0, LOCAL), BLK)
 
 
-def prefix_step(s, q_ref, paged, bias_ref, state):
-    rows, span = pl.ds(0, LOCAL), pl.ds(s * STEP_KEYS, STEP_KEYS)
+def prefix_step(start, count, q_ref, paged, bias_ref, state):
+    rows, span = pl.ds(0, LOCAL), pl.ds(start * CHUNK_KEYS, count * CHUNK_KEYS)
 
     def body(k, _):
         group_heads(k, q_ref, rows, paged[0, k, span], paged[1, k, span], state,
@@ -137,12 +136,13 @@
     lax.fori_loop(0, KVH, body, 0)
 
 
-def last_step(s, q_ref, paged, bias_ref, state, out_ref, out_sem):
-    rows, span = pl.ds(0, LOCAL), pl.ds(s * STEP_KEYS, STEP_KEYS)
-
-    def out_copy(k):
-        columns = pl.ds(pl.multiple_of(k * GROUP * HD, GROUP * HD), GROUP * HD)
-        return pltpu.make_async_copy(q_ref.at[:, columns], out_ref.at[:, columns], out_sem.at[k])
+def out_copy(k, q_ref, out_ref, out_sem):
+    columns = pl.ds(pl.multiple_of(k * GROUP * HD, GROUP * HD), GROUP * HD)
+    return pltpu.make_async_copy(q_ref.at[:, columns], out_ref.at[:, columns], out_sem.at[k])
+
+
+def last_step(part, start, count, q_ref, paged, bias_ref, state, out_ref, out_sem):
+    rows, span = pl.ds(0, LOCAL), pl.ds(start * CHUNK_KEYS, count * CHUNK_KEYS)
 
     def divide(h, result):
         out, _, total = result
@@ -151,14 +151,9 @@
 
     def body(k, _):
         group_heads(k, q_ref, rows, paged[0, k, span], paged[1, k, span], state, divide, bias=bias_ref[pl.ds(0, 1), span])
-        out_copy(k).start()
-        return 0
-    lax.fori_loop(0, KVH, body, 0)
-
-    def finish(k, _):
-        out_copy(k).wait()
-        return 0
-    lax.fori_loop(0, KVH, finish, 0)
+        out_copy(k, q_ref, out_ref, out_sem).start()
+        return 0
+    lax.fori_loop(part * KVH // 2, (part + 1) * KVH // 2, body, 0)
 
 
 def unfold(g, land, paged):
@@ -169,6 +164,15 @@
             for half in range(2):
                 part = block[:, half].reshape(CHUNK_KEYS, HD).astype(jnp.bfloat16)
                 paged[i, half * 4 + lane, pl.ds(g * CHUNK_KEYS, CHUNK_KEYS)] = part
+
+
+def unfold_direct(part, land, paged):
+    for g in DIRECT:
+        for lane in range(4):
+            block = land[part, pl.ds(g * CHUNK_ROWS, CHUNK_ROWS), lane * HD:(lane + 1) * HD]
+            block = block.astype(jnp.float32).reshape(PER_CHUNK, 2, PAGE, HD)
+            for i in range(2):
+                paged[i, part * 4 + lane, pl.ds(g * CHUNK_KEYS, CHUNK_KEYS)] = block[:, i].reshape(CHUNK_KEYS, HD).astype(jnp.bfloat16)
 
 
 def visible_bias(me, parent_ref, pages_ref, leaf_ref, length_ref, slot_ref, bias_ref):
@@ -201,8 +205,8 @@
     bias_ref[...] = jnp.broadcast_to(jnp.where(shown, 0.0, HIDDEN), bias_ref.shape)
 
 
-def kernel(parent_ref, pages_ref, leaf_ref, length_ref, slot_ref, pk_ref, pv_ref, q_hbm, sk_hbm, sv_hbm, out_ref,
-           q_ref, suf, other, land, send, paged, acc_ref, max_ref, sum_ref, bias_ref, row_vec, row_smem,
+def kernel(parent_ref, pages_ref, leaf_ref, length_ref, slot_hbm, pk_ref, pv_ref, q_hbm, sk_hbm, sv_hbm, out_ref,
+           slot_ref, q_ref, suf, other, land, send, paged, acc_ref, max_ref, sum_ref, bias_ref, row_vec, row_smem,
            load_sem, row_sem, self_sem, send_sem, recv_sem, fwd_send, fwd_recv, suf_send, suf_recv, out_sem, near):
     me = lax.axis_index("store")
     p = lax.axis_index("pair")
@@ -213,6 +217,8 @@
     def tell(sem, dy, dz, dx, dc):
         pl.semaphore_signal(sem, inc=1, device_id=(shifted(me, dy, dz, dx, dc), (p + dy) % 2), device_id_type=MESH)
 
+    load_slots = pltpu.make_async_copy(slot_hbm, slot_ref, row_sem)
+    load_slots.start()
     for dy, dx, dc in plane:
         tell(barrier, dy, 0, dx, dc)
     for dz in range(1, 8):
@@ -225,10 +231,13 @@
     for copy in loads:
         copy.start()
 
+    load_slots.wait()
     places = slot_ref[...]
     mine = jnp.where(places // PAGES_DEV == me, places % PAGES_DEV, 0)
     best = jnp.max(mine, axis=1, keepdims=True)
-    row_vec[...] = jnp.broadcast_to(best, row_vec.shape)
+    shape = (places.shape[0], 128)
+    own_lane = lax.broadcasted_iota(jnp.int32, shape, 0) == lax.broadcasted_iota(jnp.int32, shape, 1)
+    row_vec[...] = jnp.broadcast_to(jnp.sum(jnp.where(own_lane, best, 0), axis=0, keepdims=True), row_vec.shape)
     to_smem = pltpu.make_async_copy(row_vec, row_smem, row_sem)
     to_smem.start()
     to_smem.wait()
@@ -237,26 +246,31 @@
         dy, dx = chunk_step(g)
         return dy, Z_ORDER[item // 2], dx, item % 2
 
-    def pack(g, _):
+    def pack(g, direct=False):
         for item in range(PER_CHUNK):
             dy, dz, dx, dc = target(g, item)
             leaf = leaf_ref[shifted(me, dy, dz, dx, dc)]
             mid = parent_ref[leaf]
-            row = jnp.maximum(jnp.maximum(row_smem[0, 0], row_smem[1 + mid, 0]), row_smem[1 + MIDS + leaf, 0])
+            row = jnp.maximum(jnp.maximum(row_smem[0, 0], row_smem[0, 1 + mid]), row_smem[0, 1 + MIDS + leaf])
             start = pl.multiple_of(g * CHUNK_ROWS + item * ROWS, ROWS)
 
-            def put(i, page_ref):
-                page = page_ref[jnp.clip(row, 0, PAGES_DEV - 1)]
-                send[i, pl.ds(start, ROWS), :] = jnp.concatenate([page[:, :LANES], page[:, LANES:]], axis=0)
-
-            @pl.when((p == 0) | (g >= FIRST_DIRECT))
-            def _():
-                put(0, pk_ref)
-
-            @pl.when((p == 1) | (g >= FIRST_DIRECT))
-            def _():
-                put(1, pv_ref)
-        return 0
+            row = jnp.clip(row, 0, PAGES_DEV - 1)
+
+            def put(i, upper, lower):
+                send[i, pl.ds(start, ROWS), :] = jnp.concatenate([upper, lower], axis=0)
+
+            if direct:
+                keys, values = pk_ref[row], pv_ref[row]
+                put(0, keys[:, :LANES], values[:, :LANES])
+                put(1, keys[:, LANES:], values[:, LANES:])
+            else:
+                @pl.when(p == 0)
+                def _():
+                    put(0, pk_ref[row][:, :LANES], pk_ref[row][:, LANES:])
+
+                @pl.when(p == 1)
+                def _():
+                    put(1, pv_ref[row][:, :LANES], pv_ref[row][:, LANES:])
 
     def chunk_span(g):
         return pl.ds(pl.multiple_of(g * CHUNK_ROWS, CHUNK_ROWS), CHUNK_ROWS)
@@ -265,22 +279,24 @@
         span = pl.ds(SELF_ITEM * ROWS, ROWS)
         return pltpu.make_async_copy(send.at[p, span], land.at[p, span], self_sem)
 
-    def send_chunk(g, i, extra=0):
+    def send_item(g, item, i, sem=None, extra=0):
+        dy, dz, dx, dc = target(g, item)
+        span = pl.ds(pl.multiple_of(g * CHUNK_ROWS + item * ROWS, ROWS), ROWS)
+        pltpu.make_async_remote_copy(
+            send.at[i, span], land.at[i, span], send_sem.at[extra], recv_sem.at[g if sem is None else sem],
+            device_id=(shifted(me, dy, dz, dx, dc), (p + dy) % 2), device_id_type=MESH).start()
+
+    def send_chunk(g, i, sem=None, extra=0):
         for item in range(PER_CHUNK):
-            dy, dz, dx, dc = target(g, item)
-            span = pl.ds(pl.multiple_of(g * CHUNK_ROWS + item * ROWS, ROWS), ROWS)
-            copy = pltpu.make_async_remote_copy(
-                send.at[i, span], land.at[i, span], send_sem.at[extra], recv_sem.at[g],
-                device_id=(shifted(me, dy, dz, dx, dc), (p + dy) % 2), device_id_type=MESH)
-            if item == SELF_ITEM:
-                pl.when(g != 0)(copy.start)
-            else:
-                copy.start()
-
-    lax.fori_loop(0, 2, pack, 0)
+            send_item(g, item, i, sem, extra)
+
+    pack(0)
     pl.semaphore_wait(barrier, 8 + len(plane))
     for dy, dx, dc in plane:
         tell(near, dy, 0, dx, dc)
+    for item in range(0, PER_CHUNK, 2):
+        if item != SELF_ITEM:
+            send_item(0, item, p)
     loads[0].wait()
     loads[1].wait()
 
@@ -293,22 +309,30 @@
         def _():
             suffix_copy(0, rows).start()
             suffix_copy(1, rows).start()
+    own_item(0).start()
+    pack(1)
     pl.semaphore_wait(near, len(plane))
-    own_item(0).start()
+    for item in range(1, PER_CHUNK, 2):
+        send_item(0, item, p)
+    send_chunk(1, p)
 
     def pack_send(g, _):
-        @pl.when(g >= 2)
-        def _():
-            pack(g, 0)
-
+        pack(g)
         send_chunk(g, p)
-
-        @pl.when(g >= FIRST_DIRECT)
-        def _():
-            send_chunk(g, 1 - p, 1)
-        return 0
-
-    lax.fori_loop(0, CHUNKS, pack_send, 0)
+        return 0
+
+    def pack_send_lower(g, _):
+        pack(g, direct=True)
+        send_chunk(g, 0, DIRECT[0])
+        return 0
+
+    def send_upper(g, _):
+        send_chunk(g, 1, DIRECT[1], 1)
+        return 0
+
+    lax.fori_loop(2, FIRST_DIRECT, pack_send, 0)
+    lax.fori_loop(FIRST_DIRECT, CHUNKS, pack_send_lower, 0)
+    lax.fori_loop(FIRST_DIRECT, CHUNKS, send_upper, 0)
 
     def forward(g):
         q = (p + g % 2) % 2
@@ -320,18 +344,18 @@
         pltpu.make_async_copy(part, part, sem).wait()
 
     def receive(g):
-        if g in DIRECT:
-            arrived(2 * PER_CHUNK, recv_sem.at[g])
-            return
         arrived(PER_CHUNK - (g == 0), recv_sem.at[g])
         if g == 0:
             own_item(0).wait()
         forward(g).start()
 
     def whole(g):
-        if g not in DIRECT:
-            arrived(PER_CHUNK, fwd_recv.at[g])
+        arrived(PER_CHUNK, fwd_recv.at[g])
         unfold(g, land, paged)
+
+    def direct_part(part):
+        arrived(len(DIRECT) * PER_CHUNK, recv_sem.at[DIRECT[part]])
+        unfold_direct(part, land, paged)
 
     visible_bias(me, parent_ref, pages_ref, leaf_ref, length_ref, slot_ref, bias_ref)
     loads[2].wait()
@@ -348,20 +372,20 @@
     whole(0)
     receive(3)
     whole(1)
-    prefix_step(0, q_ref, paged, bias_ref, state)
+    prefix_step(0, 2, q_ref, paged, bias_ref, state)
     receive(4)
     whole(2)
     receive(5)
     whole(3)
-    prefix_step(1, q_ref, paged, bias_ref, state)
+    prefix_step(2, 2, q_ref, paged, bias_ref, state)
     whole(4)
     whole(5)
-    prefix_step(2, q_ref, paged, bias_ref, state)
-    receive(6)
-    whole(6)
-    receive(7)
-    whole(7)
-    last_step(3, q_ref, paged, bias_ref, state, out_ref, out_sem)
+    prefix_step(4, 2, q_ref, paged, bias_ref, state)
+    for part in range(2):
+        direct_part(part)
+        last_step(part, 6, 2, q_ref, paged, bias_ref, state, out_ref, out_sem)
+    for k in range(KVH):
+        out_copy(k, q_ref, out_ref, out_sem).wait()
 
     for g in range(CHUNKS):
         if g not in DIRECT:
@@ -381,13 +405,13 @@
     anywhere = pl.BlockSpec(memory_space=pl.ANY)
     bf16, f32 = jnp.bfloat16, jnp.float32
     dma = pltpu.SemaphoreType.DMA
-    nodes = page_slot.shape[0]
     out = pl.pallas_call(
         kernel,
         out_shape=jax.ShapeDtypeStruct((LOCAL, QH * HD), bf16),
-        in_specs=[smem] * 4 + [vmem] * 3 + [anywhere] * 3,
+        in_specs=[smem] * 4 + [anywhere] + [vmem] * 2 + [anywhere] * 3,
         out_specs=anywhere,
         scratch_shapes=[
+            pltpu.VMEM(page_slot.shape, jnp.int32),
             pltpu.VMEM((LOCAL, QH * HD), bf16),
             pltpu.VMEM((2, LOCAL, KVH * HD), bf16),
             pltpu.VMEM((2, LOCAL, KVH * HD), bf16),
@@ -398,8 +422,8 @@
             pltpu.VMEM((QH, LOCAL, HD), f32),
             pltpu.VMEM((QH, LOCAL, HD), f32),
             pltpu.VMEM((8, SLOTS * PAGE), f32),
-            pltpu.VMEM((nodes, 128), jnp.int32),
-            pltpu.SMEM((nodes, 128), jnp.int32),
+            pltpu.VMEM((8, 128), jnp.int32),
+            pltpu.SMEM((8, 128), jnp.int32),
             dma((3,)), dma, dma, dma((2,)), dma((CHUNKS,)), dma((CHUNKS,)), dma((CHUNKS,)), dma((2,)), dma((2,)), dma((KVH,)),
             pltpu.SemaphoreType.REGULAR,
         ],

time: 93.7 us -> 95.9 us (1.023)
  Pallas kernels: 87.3 us -> 89.6 us
    pallas_call x1, Pallas kernels: 87.3 us -> 89.6 us  [local(): pl.pallas_call(kernel, out_shape=jax.ShapeDtypeStruct((LOCAL, QH * HD), b...]
where the time goes in v3:
time: 95.9 us; the launch traced here: 95.7 us
  Pallas kernels  89.6 us (93%)
  local copies, waits for them, and re-layouts  6.11 us (6%)
    pallas_call x1, Pallas kernels, local(): pl.pallas_call(kernel, out_shape=jax.ShapeDtypeStruct((LOCAL, QH * HD), b...  89.6 us
    unnamed x2, local copies, waits for them, and re-layouts  6.11 us

profile of v3, /device:TPU:1, one launch (start us, length us, event | category | flops | bytes accessed | tf_op | source)
XLA Modules:
  0.0 95.7 jit_solution(17066540274008539381)
XLA Ops:
  0.0 1.5 %copy.11.slot_hbm = s32[81,64]{1,0:T(8,128)} copy(s32[81,64]{0,1:T(8,128)} %param.17) | data formatting | bytes 41472 | tf_op args[7]
  1.5 89.6 %shard_map.100 = bf16[256,8192]{1,0:T(8,128)(2,1)} custom-call(s32[64]{0:T(128)} %parent_ref.1, s32[81]{0:T(128)} %pages_ref.1, s32[128]{0:T(128)} %leaf_ref.1, s32[128]{0:T(128)} %length_ref.1, s32[81,64]{1,0:T(8,128)} %copy.11.slot_hbm, bf16[64,8,1024]{2,1,0:T(8,128)(2,1)} %pk_ref.1, bf16[64,8,1024]{2,1,0:T(8,128)(2,1)} %pv_ref.1, ...), custom_call_target="tpu_custom_call" | custom-call | tf_op jit(solution)/shard_map/pallas_call | solution.py:408
  91.0 4.6 %copy.13 = bf16[1,1,2,128,8192]{4,3,2,1,0:T(8,128)(2,1)} copy(bf16[1,1,2,128,8192]{4,3,2,1,0:T(8,128)(2,1)} %bitcast.4) | data formatting | bytes 8388608

commit v4 on v3

--- a/solution.py
+++ b/solution.py
@@ -31,12 +31,12 @@
 
 
 def shifted(me, dy, dz, dx, dc):
-    yh, z, x, c = me // 64, me // 8 % 8, me // 2 % 4, me % 2
-    return (((yh + dy) % 2 * 8 + (z + dz) % 8) * 4 + (x + dx) % 4) * 2 + (c + dc) % 2
+    yh, z, x, c = (me >> 6) + dy, (me >> 3) + dz, (me >> 1) + dx, me + dc
+    return ((yh & 1) << 6) + ((z & 7) << 3) + ((x & 3) << 1) + (c & 1)
 
 
 def chunk_step(g):
-    return g % 2, g // 2
+    return g & 1, g >> 1
 
 
 def score(q, keys):
@@ -181,10 +181,10 @@
     length = length_ref[me]
     width = slot_ref.shape[1]
     key = lax.broadcasted_iota(jnp.int32, (1, SLOTS * PAGE), 1)
-    d = key // PAGE
-    g, item = d // PER_CHUNK, d % PER_CHUNK
-    iz, dc = item // 2, item % 2
-    dz = jnp.where(iz % 2 == 0, iz // 2 + 1, (8 - iz // 2) % 8)
+    d = key >> 3
+    g, item = d >> 4, d & 15
+    iz, dc = item >> 1, item & 1
+    dz = jnp.where((iz & 1) == 0, (iz >> 1) + 1, (8 - (iz >> 1)) & 7)
     dy, dx = chunk_step(g)
     holder = shifted(me + jnp.zeros_like(key), 2 - dy, 8 - dz, 4 - dx, 2 - dc).astype(jnp.float32)
     across = lax.broadcasted_iota(jnp.int32, (width, width), 1)
@@ -194,14 +194,14 @@
     first = 0
     for node in (0, 1 + mid, 1 + MIDS + leaf):
         count = pages_ref[node]
-        row = (slot_ref[pl.ds(node, 1), :] // PAGES_DEV).astype(jnp.float32)
+        row = (slot_ref[pl.ds(node, 1), :] >> 6).astype(jnp.float32)
         column = jnp.sum(jnp.where(across == down, jnp.broadcast_to(row, (width, width)), 0.0), axis=1, keepdims=True)
         tokens = jnp.clip(length - PAGE * (first + order), 0, PAGE)
         tokens = jnp.where(order < count, tokens, 0).astype(jnp.float32)
         match = column == holder
         seen = seen + jnp.sum(jnp.where(match, tokens, 0.0), axis=0, keepdims=True)
         first = first + count
-    shown = (key % PAGE).astype(jnp.float32) < seen
+    shown = (key & 7).astype(jnp.float32) < seen
     bias_ref[...] = jnp.broadcast_to(jnp.where(shown, 0.0, HIDDEN), bias_ref.shape)
 
 
@@ -215,7 +215,7 @@
     plane = [(dy, dx, dc) for dy in range(2) for dx in range(4) for dc in range(2) if (dy, dx, dc) != (0, 0, 0)]
 
     def tell(sem, dy, dz, dx, dc):
-        pl.semaphore_signal(sem, inc=1, device_id=(shifted(me, dy, dz, dx, dc), (p + dy) % 2), device_id_type=MESH)
+        pl.semaphore_signal(sem, inc=1, device_id=(shifted(me, dy, dz, dx, dc), (p + dy) & 1), device_id_type=MESH)
 
     load_slots = pltpu.make_async_copy(slot_hbm, slot_ref, row_sem)
     load_slots.start()
@@ -233,7 +233,7 @@
 
     load_slots.wait()
     places = slot_ref[...]
-    mine = jnp.where(places // PAGES_DEV == me, places % PAGES_DEV, 0)
+    mine = jnp.where(places >> 6 == me, places & 63, 0)
     best = jnp.max(mine, axis=1, keepdims=True)
     shape = (places.shape[0], 128)
     own_lane = lax.broadcasted_iota(jnp.int32, shape, 0) == lax.broadcasted_iota(jnp.int32, shape, 1)
@@ -242,35 +242,39 @@
     to_smem.start()
     to_smem.wait()
 
-    def target(g, item):
+    near_part = [shifted(me & 57, 0, Z_ORDER[item // 2], 0, item % 2) for item in range(PER_CHUNK)]
+
+    def chunk_target(g):
         dy, dx = chunk_step(g)
-        return dy, Z_ORDER[item // 2], dx, item % 2
+        return shifted(me & 70, dy, 0, dx, 0), (p + dy) & 1
 
     def pack(g, direct=False):
-        for item in range(PER_CHUNK):
-            dy, dz, dx, dc = target(g, item)
-            leaf = leaf_ref[shifted(me, dy, dz, dx, dc)]
-            mid = parent_ref[leaf]
-            row = jnp.maximum(jnp.maximum(row_smem[0, 0], row_smem[0, 1 + mid]), row_smem[0, 1 + MIDS + leaf])
+        far_part, _ = chunk_target(g)
+
+        def put(i, item, upper, lower):
             start = pl.multiple_of(g * CHUNK_ROWS + item * ROWS, ROWS)
-
-            row = jnp.clip(row, 0, PAGES_DEV - 1)
-
-            def put(i, upper, lower):
-                send[i, pl.ds(start, ROWS), :] = jnp.concatenate([upper, lower], axis=0)
-
-            if direct:
+            send[i, pl.ds(start, ROWS), :] = jnp.concatenate([upper, lower], axis=0)
+
+        def rows():
+            for item in range(PER_CHUNK):
+                leaf = leaf_ref[far_part + near_part[item]]
+                mid = parent_ref[leaf]
+                row = jnp.maximum(jnp.maximum(row_smem[0, 0], row_smem[0, 1 + mid]), row_smem[0, 1 + MIDS + leaf])
+                yield item, jnp.clip(row, 0, PAGES_DEV - 1)
+
+        if direct:
+            for item, row in rows():
                 keys, values = pk_ref[row], pv_ref[row]
-                put(0, keys[:, :LANES], values[:, :LANES])
-                put(1, keys[:, LANES:], values[:, LANES:])
-            else:
-                @pl.when(p == 0)
-                def _():
-                    put(0, pk_ref[row][:, :LANES], pk_ref[row][:, LANES:])
-
-                @pl.when(p == 1)
-                def _():
-                    put(1, pv_ref[row][:, :LANES], pv_ref[row][:, LANES:])
+                put(0, item, keys[:, :LANES], values[:, :LANES])
+                put(1, item, keys[:, LANES:], values[:, LANES:])
+            return
+
+        for i, page_ref in ((0, pk_ref), (1, pv_ref)):
+            @pl.when(p == i)
+            def _():
+                for item, row in rows():
+                    page = page_ref[row]
+                    put(i, item, page[:, :LANES], page[:, LANES:])
 
     def chunk_span(g):
         return pl.ds(pl.multiple_of(g * CHUNK_ROWS, CHUNK_ROWS), CHUNK_ROWS)
@@ -280,11 +284,11 @@
         return pltpu.make_async_copy(send.at[p, span], land.at[p, span], self_sem)
 
     def send_item(g, item, i, sem=None, extra=0):
-        dy, dz, dx, dc = target(g, item)
+        far_part, to_pair = chunk_target(g)
         span = pl.ds(pl.multiple_of(g * CHUNK_ROWS + item * ROWS, ROWS), ROWS)
         pltpu.make_async_remote_copy(
             send.at[i, span], land.at[i, span], send_sem.at[extra], recv_sem.at[g if sem is None else sem],
-            device_id=(shifted(me, dy, dz, dx, dc), (p + dy) % 2), device_id_type=MESH).start()
+            device_id=(far_part + near_part[item], to_pair), device_id_type=MESH).start()
 
     def send_chunk(g, i, sem=None, extra=0):
         for item in range(PER_CHUNK):
@@ -335,7 +339,7 @@
     lax.fori_loop(FIRST_DIRECT, CHUNKS, send_upper, 0)
 
     def forward(g):
-        q = (p + g % 2) % 2
+        q = (p + g) & 1
         part = land.at[q, chunk_span(g)]
         return pltpu.make_async_remote_copy(part, part, fwd_send.at[g], fwd_recv.at[g], device_id=(me, 1 - p), device_id_type=MESH)
 

time: 95.9 us -> 95.7 us (level)
  no operation moved by 1% of the time
where the time goes in v4:
time: 95.7 us; the launch traced here: 95.5 us
  Pallas kernels  89.4 us (93%)
  local copies, waits for them, and re-layouts  6.11 us (6%)
    pallas_call x1, Pallas kernels, local(): pl.pallas_call(kernel, out_shape=jax.ShapeDtypeStruct((LOCAL, QH * HD), b...  89.4 us
    unnamed x2, local copies, waits for them, and re-layouts  6.11 us

profile of v4, /device:TPU:1, one launch (start us, length us, event | category | flops | bytes accessed | tf_op | source)
XLA Modules:
  0.0 95.5 jit_solution(13564441779273616336)
XLA Ops:
  0.0 1.5 %copy.11.slot_hbm = s32[81,64]{1,0:T(8,128)} copy(s32[81,64]{0,1:T(8,128)} %param.17) | data formatting | bytes 41472 | tf_op args[7]
  1.5 89.4 %shard_map.100 = bf16[256,8192]{1,0:T(8,128)(2,1)} custom-call(s32[64]{0:T(128)} %parent_ref.1, s32[81]{0:T(128)} %pages_ref.1, s32[128]{0:T(128)} %leaf_ref.1, s32[128]{0:T(128)} %length_ref.1, s32[81,64]{1,0:T(8,128)} %copy.11.slot_hbm, bf16[64,8,1024]{2,1,0:T(8,128)(2,1)} %pk_ref.1, bf16[64,8,1024]{2,1,0:T(8,128)(2,1)} %pv_ref.1, ...), custom_call_target="tpu_custom_call" | custom-call | tf_op jit(solution)/shard_map/pallas_call | solution.py:412
  90.8 4.6 %copy.13 = bf16[1,1,2,128,8192]{4,3,2,1,0:T(8,128)(2,1)} copy(bf16[1,1,2,128,8192]{4,3,2,1,0:T(8,128)(2,1)} %bitcast.4) | data formatting | bytes 8388608
